TPU v7x, 128 devices: a whole 4x4x4 slice. The times are simulated.
128 devices in a mesh: sub: 16 (over z, x), blk: 8 (over y, core).
Axes of the slice: x: 4, y: 4, z: 4, core: 2. Of those that a mesh axis runs over, the one named last changes fastest.
Arguments:
- right_side: float32 [64, 2048, 512], P('sub', 'blk'), may hold values from -8 to 8
- trans_x: float32 [64, 2048, 512], P('sub', 'blk'), may hold values from 0.01 to 10
- trans_y: float32 [64, 2048, 512], P('sub', 'blk'), may hold values from 0.01 to 10
- trans_z: float32 [64, 2048, 512], P('sub', 'blk'), may hold values from 0.01 to 10
- storage: float32 [64, 2048, 512], P('sub', 'blk'), may hold values from 0.05 to 1
- pair_perm: int32 [16, 8, 1024], P('sub', 'blk'), may hold values from 0 to 1023, each once within a row
- pair_type: int32 [16, 8, 1024], P('sub', 'blk'), may hold values from 0 to 3
- pair_count: int32 [16, 8], P('sub', 'blk'), may hold values from 256 to 1024
- proj: float32 [4, 128, 128], replicated, may hold values from -1 to 2, as said below
Outputs:
- solution_field: float32 [64, 2048, 512], P('sub', 'blk')
- residual: float32 [64, 2048, 512], P('sub', 'blk')
Inputs may be any that keep to these rules, and one draw needn't show every extreme that they name: `pair_perm`: each subdomain's list is a permutation of its face blocks. `proj`: projection matrices of order one.
All inputs are finite; a program needn't handle non-finite values.
Results may differ from a plain program's by a relative error of at most 0.00013.
Values sent between devices are 32-bit elements; how exact they have to be, the bound alone decides.
A program may use at most 128 MiB of HBM per device.

v0:
```python
import jax
import jax.numpy as jnp
from jax import lax
from jax.sharding import PartitionSpec as P

ITERS = 2


penalty = 4.0


def shifted(array, axis, by):
    size = lax.axis_size(axis)
    pairs = [(i, i + by) for i in range(size) if 0 <= i + by < size]
    return lax.ppermute(array, axis, pairs)


def with_halo(block, sides, width):
    for axis, dim in sides:
        count = lax.axis_size(axis)
        forward = [(i, i + 1) for i in range(count - 1)]
        backward = [(target, source) for source, target in forward]
        low = lax.ppermute(
            lax.slice_in_dim(block, block.shape[dim] - width, None, axis=dim), axis, forward
        )
        high = lax.ppermute(lax.slice_in_dim(block, 0, width, axis=dim), axis, backward)
        block = jnp.concatenate([low, block, high], axis=dim)
    return block


def mortar_jump(last_face, gathered, selects, live, proj):
    projected = jnp.zeros_like(last_face)
    for kind in range(len(selects)):
        projected = projected + selects[kind] * jnp.einsum(
            "kc,ac->ka", gathered, proj[kind], precision=lax.Precision.HIGHEST
        )
    return live * (last_face - projected)


def mortar_back(jump, selects, proj):
    back = jnp.zeros_like(jump)
    for kind in range(len(selects)):
        back = back + selects[kind] * jnp.einsum(
            "ka,ac->kc", jump, proj[kind], precision=lax.Precision.HIGHEST
        )
    return -penalty * back


def body(right_side, trans_x, trans_y, trans_z, storage, pair_perm, pair_type, pair_count, proj):
    cells_x, cells_y, cells_z = right_side.shape
    blocks = pair_perm.shape[2]
    width = proj.shape[1]
    kinds_total = proj.shape[0]
    total_y = cells_y * lax.axis_size("blk")
    x_index = jnp.arange(cells_x, dtype=jnp.int32)[:, None, None]
    y_index = lax.axis_index("blk") * cells_y + jnp.arange(cells_y, dtype=jnp.int32)[None, :, None]
    z_index = jnp.arange(cells_z, dtype=jnp.int32)[None, None, :]
    coeff_x = trans_x * (x_index != cells_x - 1).astype(jnp.float32)
    coeff_y = trans_y * (y_index != total_y - 1).astype(jnp.float32)
    coeff_z = trans_z * (z_index != cells_z - 1).astype(jnp.float32)
    below = shifted(coeff_y[:, cells_y - 1 :, :], "blk", 1)
    prev_y = jnp.concatenate([below, coeff_y[:, : cells_y - 1]], 1)
    prev_x = jnp.concatenate([jnp.zeros_like(coeff_x[:1]), coeff_x[: cells_x - 1]], 0)
    prev_z = jnp.concatenate([jnp.zeros_like(coeff_z[:, :, :1]), coeff_z[:, :, : cells_z - 1]], 2)
    partner = pair_perm[0, 0]
    kinds = pair_type[0, 0]
    block_ids = jnp.arange(blocks, dtype=jnp.int32)
    live = (block_ids < pair_count[0, 0]).astype(jnp.float32)[:, None]
    selects = [(kinds == kind).astype(jnp.float32)[:, None] for kind in range(kinds_total)]

    def squares(values):
        return lax.psum(jnp.sum(values * values), ("sub", "blk"))

    solution_field = jnp.zeros_like(right_side)
    residual = right_side
    direction = right_side
    norm_now = squares(residual)
    for step in range(ITERS):
        padded = with_halo(direction, (("blk", 1),), 1)
        next_y = padded[:, 2:]
        before_y = padded[:, :-2]
        next_x = jnp.concatenate([direction[1:], jnp.zeros_like(direction[:1])], 0)
        before_x = jnp.concatenate([jnp.zeros_like(direction[:1]), direction[:-1]], 0)
        next_z = jnp.concatenate([direction[:, :, 1:], jnp.zeros_like(direction[:, :, :1])], 2)
        before_z = jnp.concatenate([jnp.zeros_like(direction[:, :, :1]), direction[:, :, :-1]], 2)
        result = storage * direction
        result = result + coeff_x * (direction - next_x) + prev_x * (direction - before_x)
        result = result + coeff_y * (direction - next_y) + prev_y * (direction - before_y)
        result = result + coeff_z * (direction - next_z) + prev_z * (direction - before_z)
        last_face = direction[cells_x - 1].reshape(blocks, width)
        first_face = direction[0].reshape(blocks, width)
        right_face = shifted(first_face, "sub", -1)
        jump = mortar_jump(last_face, jnp.take(right_face, partner, axis=0), selects, live, proj)
        back = mortar_back(jump, selects, proj)
        ordered = jnp.zeros_like(back).at[partner].set(back)
        received = shifted(ordered, "sub", 1)
        result = result.at[cells_x - 1].add((penalty * jump).reshape(cells_y, cells_z))
        result = result.at[0].add(received.reshape(cells_y, cells_z))
        alpha = norm_now / lax.psum(jnp.sum(direction * result), ("sub", "blk"))
        solution_field = solution_field + alpha * direction
        residual = residual - alpha * result
        norm_next = squares(residual)
        direction = residual + norm_next / norm_now * direction
        norm_now = norm_next
    return (solution_field, residual)


def solution(mesh):
    in_specs = (
        P("sub", "blk", None),
        P("sub", "blk", None),
        P("sub", "blk", None),
        P("sub", "blk", None),
        P("sub", "blk", None),
        P("sub", "blk", None),
        P("sub", "blk", None),
        P("sub", "blk"),
        P(),
    )
    out_specs = (P("sub", "blk", None), P("sub", "blk", None))
    return jax.shard_map(body, mesh=mesh, in_specs=in_specs, out_specs=out_specs, check_vma=False)
```

profile of v0, /device:TPU:1, one launch (start us, length us, event | category | flops | bytes accessed | tf_op | source)
XLA Modules:
  0.0 333.2 jit_solution(610079607642793674)
XLA Ops:
  0.6 0.9 fusion.118
  1.5 4.6 %collective-permute-start.2 = (f32[4,1,512]{2,1,0:T(1,128)S(1)}, f32[4,1,512]{2,1,0:T(1,128)S(1)}, u32[]{:S(2)}, u32[]{:S(2)}) collective-permute-start(f32[4,1,512]{2,1,0:T(1,128)S(1)} %get-tuple-element.72), channel_id=1, source_target_pairs={{0,1},{1,2},{2,3},{3,4},{4,5},{5,6},{6,7},{8,9},{9,10},{10,11},{11... | collective-permute-start | bytes 24584 | tf_op jit(solution)/shard_map/ppermute | solution.py:23
  6.1 1.9 collective-permute-start
  8.1 1.9 broadcast_multiply_fusion.1
  10.0 1.3 copy-done.3
  11.4 3.6 %collective-permute-start.1 = (f32[4,1,512]{2,1,0:T(1,128)S(1)}, f32[4,1,512]{2,1,0:T(1,128)S(1)}, u32[]{:S(2)}, u32[]{:S(2)}) collective-permute-start(f32[4,1,512]{2,1,0:T(1,128)S(1)} %slice.225), channel_id=1, source_target_pairs={{0,1},{1,2},{2,3},{3,4},{4,5},{5,6},{6,7},{8,9},{9,10},{10,11},{11... | collective-permute-start | bytes 24584 | tf_op jit(solution)/shard_map/ppermute | solution.py:15
  15.1 0.9 reshape_squeeze.13
  16.0 1.3 collective-permute-start.3
  17.3 2.2 fusion.116
  19.6 1.1 copy-done.6
  20.6 2.0 broadcast_multiply_fusion
  22.7 1.3 copy-done.2
  24.0 1.3 slice.224
  25.2 0.9 reshape_squeeze.12
  26.8 2.8 fusion.117
  29.6 1.3 collective-permute-done.3
  30.9 2.8 gather_fusion
  33.8 0.6 convolution_multiply_fusion.12
  34.4 0.6 convolution_multiply_fusion.13
  35.0 0.6 convolution_multiply_fusion.14
  35.7 2.1 broadcast_multiply_fusion.4
  37.8 0.6 convolution_multiply_fusion.11
  38.3 0.6 fusion.28
  38.9 0.6 fusion.27
  39.5 0.6 fusion.26
  40.1 3.9 %scatter_custom_fusion = f32[1024,128]{1,0:T(8,128)} fusion(s32[1024]{0:T(1024)S(1)} %bitcast.82, f32[1024,128]{1,0:T(8,128)S(1)} %fusion.26, f32[]{:T(128)} %constant.121.clone.1), kind=kCustom, calls=%fused_computation.100 | custom fusion | bytes 524292 | tf_op jit(solution)/shard_map/scatter | solution.py:95
  44.0 3.9 %collective-permute-start.4 = (f32[1024,128]{1,0:T(8,128)}, f32[1024,128]{1,0:T(8,128)}, u32[]{:S(2)}, u32[]{:S(2)}) collective-permute-start(f32[1024,128]{1,0:T(8,128)} %scatter_custom_fusion), channel_id=1, source_target_pairs={{0,8},{8,16},{16,24},{24,32},{32,40},{40,48},{48,56},{56,64},{64,7... | collective-permute-start | bytes 1572872 | tf_op jit(solution)/shard_map/ppermute | solution.py:15
  47.9 10.3 %fusion.4 = f32[4,256,512]{2,1,0:T(8,128)} fusion(f32[3,256,512]{2,1,0:T(8,128)} %slice.224, f32[4,256,512]{2,1,0:T(8,128)S(1)} %copy-done, f32[4,1,512]{2,1,0:T(1,128)S(1)} %collective-permute-done.2, f32[4,1,512]{2,1,0:T(1,128)S(1)} %collective-permute-done, f32[4,256,511]{2,1,0:T(8,128)} %get-tuple-element.70, f32[4,256,512]{2,1,0:T(8,128)} %get-tuple-element.81, ...), kind=kLoop, calls=%fused_computation.10 | loop fusion | flops 12058624 | bytes 25695232 | tf_op jit(solution)/shard_map/add | solution.py:89
  58.2 0.1 reshape.229
  58.3 1.9 fusion.39
  60.2 1.1 reshape.230
  61.3 2.0 fusion.38
  63.3 2.7 multiply_reduce_fusion.2
  66.0 69.4 %all-reduce.10 = (f32[]{:T(128)}, f32[]{:T(128)}) all-reduce(f32[]{:T(128)} %get-tuple-element.52, f32[]{:T(128)} %get-tuple-element.51), channel_id=1, replica_groups=mesh['sub'=16,'blk'=8] {'sub','blk'}, use_global_device_ids=true, to_apply=%region_1.0 | all-reduce | flops 2 | bytes 16 | tf_op jit(solution)/shard_map/psum | solution.py:72
  136.8 2.7 multiply_reduce_fusion.1
  139.5 62.6 %psum.30 = f32[]{:T(128)} all-reduce(f32[]{:T(128)} %multiply_reduce_fusion.1), channel_id=1, replica_groups=mesh['sub'=16,'blk'=8] {'sub','blk'}, use_global_device_ids=true, to_apply=%region_6.8 | all-reduce | flops 1 | bytes 8 | tf_op jit(solution)/shard_map/psum | solution.py:72
  203.4 2.1 multiply_add_fusion.1
  205.6 2.3 fusion.112
  208.0 0.9 reshape_squeeze.15
  208.8 1.3 collective-permute-start.7
  210.1 0.9 fusion.114
  211.0 3.6 %collective-permute-start.6 = (f32[4,1,512]{2,1,0:T(1,128)S(1)}, f32[4,1,512]{2,1,0:T(1,128)S(1)}, u32[]{:S(2)}, u32[]{:S(2)}) collective-permute-start(f32[4,1,512]{2,1,0:T(1,128)S(1)} %get-tuple-element.64), channel_id=1, source_target_pairs={{0,1},{1,2},{2,3},{3,4},{4,5},{5,6},{6,7},{8,9},{9,10},{10,11},{11... | collective-permute-start | bytes 24584 | tf_op jit(solution)/shard_map/ppermute | solution.py:23
  214.6 1.9 collective-permute-start.5
  216.5 0.8 reshape_squeeze.14
  217.4 4.9 %fusion.113 = (f32[4,256,511]{2,1,0:T(8,128)}, f32[4,256,511]{2,1,0:T(8,128)}) fusion(f32[4,256,512]{2,1,0:T(8,128)} %copy-done.1), kind=kLoop, calls=%fused_computation.168 | loop fusion | bytes 8372224 | tf_op jit(solution)/shard_map/slice | solution.py:84
  222.3 1.6 collective-permute-done.7
  223.9 2.8 gather_fusion.1
  226.7 0.6 convolution_multiply_fusion.4
  227.3 0.6 convolution_multiply_fusion.5
  228.0 0.6 convolution_multiply_fusion.6
  228.6 2.1 broadcast_multiply_fusion.3
  230.7 0.6 convolution_multiply_fusion.3
  231.3 0.6 fusion.21
  231.8 0.6 fusion.20
  232.4 0.6 fusion.19
  233.0 3.9 %scatter_custom_fusion.1 = f32[1024,128]{1,0:T(8,128)} fusion(s32[1024]{0:T(1024)S(1)} %bitcast.83, f32[1024,128]{1,0:T(8,128)S(1)} %fusion.19, f32[]{:T(128)} %constant.121.clone.1), kind=kCustom, calls=%fused_computation.98 | custom fusion | bytes 524292 | tf_op jit(solution)/shard_map/scatter | solution.py:95
  236.9 3.5 %collective-permute-start.8 = (f32[1024,128]{1,0:T(8,128)}, f32[1024,128]{1,0:T(8,128)}, u32[]{:S(2)}, u32[]{:S(2)}) collective-permute-start(f32[1024,128]{1,0:T(8,128)} %scatter_custom_fusion.1), channel_id=1, source_target_pairs={{0,8},{8,16},{16,24},{24,32},{32,40},{40,48},{48,56},{56,64},{64,7... | collective-permute-start | bytes 1572872 | tf_op jit(solution)/shard_map/ppermute | solution.py:15
  240.4 12.2 %fusion.9 = f32[4,256,512]{2,1,0:T(8,128)} fusion(f32[3,256,512]{2,1,0:T(8,128)} %slice.224, f32[4,256,512]{2,1,0:T(8,128)} %copy-done.1, f32[4,1,512]{2,1,0:T(1,128)S(1)} %collective-permute-done.6, f32[4,1,512]{2,1,0:T(1,128)S(1)} %collective-permute-done.5, f32[4,256,511]{2,1,0:T(8,128)} %get-tuple-element.62, f32[4,256,512]{2,1,0:T(8,128)} %get-tuple-element.81, ...), kind=kLoop, calls=%fused_computation.15 | loop fusion | flops 12058624 | bytes 25695232 | tf_op jit(solution)/shard_map/add | solution.py:89
  252.7 1.9 fusion.37
  254.6 1.1 reshape.232
  255.8 1.9 fusion.36
  257.7 3.4 %multiply_reduce_fusion = f32[]{:T(128)} fusion(f32[4,256,512]{2,1,0:T(8,128)} %copy-done.1, f32[4,256,512]{2,1,0:T(8,128)} %fusion.36), kind=kLoop, calls=%fused_computation.31 | loop fusion | flops 1048575 | bytes 4194308 | tf_op jit(solution)/shard_map/reduce_sum | solution.py:99
  261.0 65.0 %psum.31 = f32[]{:T(128)} all-reduce(f32[]{:T(128)} %multiply_reduce_fusion), channel_id=1, replica_groups=mesh['sub'=16,'blk'=8] {'sub','blk'}, use_global_device_ids=true, to_apply=%region_9.11 | all-reduce | flops 1 | bytes 8 | tf_op jit(solution)/shard_map/psum | solution.py:99
  327.2 6.0 %multiply_subtract_fusion = (f32[4,256,512]{2,1,0:T(8,128)}, f32[4,256,512]{2,1,0:T(8,128)}) fusion(f32[4,256,512]{2,1,0:T(8,128)} %fusion.36, f32[]{:T(128)S(6)} %div.11, f32[4,256,512]{2,1,0:T(8,128)S(1)} %copy-done, f32[4,256,512]{2,1,0:T(8,128)} %fusion.38, f32[]{:T(128)S(6)} %div.9, f32[4,256,512]{2,1,0:T(8,128)} %copy-done.1), kind=kLoop, calls=%fused_computation.29 | loop fusion | flops 3670016 | bytes 12582920 | tf_op jit(solution)/shard_map/sub | solution.py:101
  (41 shorter events, 0.4 us)
Async XLA Ops:
  1.5 46.4 %collective-permute-start.2 = (f32[4,1,512]{2,1,0:T(1,128)S(1)}, f32[4,1,512]{2,1,0:T(1,128)S(1)}, u32[]{:S(2)}, u32[]{:S(2)}) collective-permute-start(f32[4,1,512]{2,1,0:T(1,128)S(1)} %get-tuple-element.72), channel_id=1, source_target_pairs={{0,1},{1,2},{2,3},{3,4},{4,5},{5,6},{6,7},{8,9},{9,10},{10,11},{11... | collective-permute-start | bytes 24584 | tf_op jit(solution)/shard_map/ppermute | solution.py:23
  6.1 41.8 %collective-permute-start = (f32[4,1,512]{2,1,0:T(1,128)S(1)}, f32[4,1,512]{2,1,0:T(1,128)S(1)}, u32[]{:S(2)}, u32[]{:S(2)}) collective-permute-start(f32[4,1,512]{2,1,0:T(1,128)S(1)} %get-tuple-element.71), channel_id=1, source_target_pairs={{1,0},{2,1},{3,2},{4,3},{5,4},{6,5},{7,6},{9,8},{10,9},{11,10},{12... | collective-permute-start | bytes 24584 | tf_op jit(solution)/shard_map/ppermute | solution.py:26
  8.1 7.0 %copy-start = (f32[4,256,512]{2,1,0:T(8,128)S(1)}, f32[4,256,512]{2,1,0:T(8,128)}, u32[]{:S(2)}) copy-start(f32[4,256,512]{2,1,0:T(8,128)} %param.19) | copy-start | bytes 6291460
  10.0 1.3 copy-start.3
  11.4 36.5 %collective-permute-start.1 = (f32[4,1,512]{2,1,0:T(1,128)S(1)}, f32[4,1,512]{2,1,0:T(1,128)S(1)}, u32[]{:S(2)}, u32[]{:S(2)}) collective-permute-start(f32[4,1,512]{2,1,0:T(1,128)S(1)} %slice.225), channel_id=1, source_target_pairs={{0,1},{1,2},{2,3},{3,4},{4,5},{5,6},{6,7},{8,9},{9,10},{10,11},{11... | collective-permute-start | bytes 24584 | tf_op jit(solution)/shard_map/ppermute | solution.py:15
  16.0 15.0 %collective-permute-start.3 = (f32[1024,128]{1,0:T(8,128)}, f32[1024,128]{1,0:T(8,128)S(1)}, u32[]{:S(2)}, u32[]{:S(2)}) collective-permute-start(f32[1024,128]{1,0:T(8,128)} %reshape_squeeze.13), channel_id=1, source_target_pairs={{8,0},{16,8},{24,16},{32,24},{40,32},{48,40},{56,48},{64,56},{72,6... | collective-permute-start | bytes 1572872 | tf_op jit(solution)/shard_map/ppermute | solution.py:15
  17.3 2.3 copy-start.5
  17.3 3.4 %copy-start.6 = (f32[4,256,512]{2,1,0:T(8,128)S(1)}, f32[4,256,512]{2,1,0:T(8,128)}, u32[]{:S(2)}) copy-start(f32[4,256,512]{2,1,0:T(8,128)} %param.20) | copy-start | bytes 6291460
  22.7 1.3 copy-start.2
  24.0 2.1 copy-start.11
  24.0 2.2 copy-start.12
  29.6 4.2 %copy-start.4 = (f32[4,128,128]{2,1,0:T(8,128)S(1)}, f32[4,128,128]{2,1,0:T(8,128)}, u32[]{:S(2)}) copy-start(f32[4,128,128]{2,1,0:T(8,128)} %param.27) | copy-start | bytes 786436
  33.8 1.9 copy-start.9
  44.0 16.2 %collective-permute-start.4 = (f32[1024,128]{1,0:T(8,128)}, f32[1024,128]{1,0:T(8,128)}, u32[]{:S(2)}, u32[]{:S(2)}) collective-permute-start(f32[1024,128]{1,0:T(8,128)} %scatter_custom_fusion), channel_id=1, source_target_pairs={{0,8},{8,16},{16,24},{24,32},{32,40},{40,48},{48,56},{56,64},{64,7... | collective-permute-start | bytes 1572872 | tf_op jit(solution)/shard_map/ppermute | solution.py:15
  47.9 10.3 %copy-start.8 = (f32[1024,128]{1,0:T(8,128)S(1)}, f32[1024,128]{1,0:T(8,128)}, u32[]{:S(2)}) copy-start(f32[1024,128]{1,0:T(8,128)} %get-tuple-element.77) | copy-start | bytes 1572868
  205.5 2.3 copy-start.1
  208.8 15.0 %collective-permute-start.7 = (f32[1024,128]{1,0:T(8,128)}, f32[1024,128]{1,0:T(8,128)S(1)}, u32[]{:S(2)}, u32[]{:S(2)}) collective-permute-start(f32[1024,128]{1,0:T(8,128)} %reshape_squeeze.15), channel_id=1, source_target_pairs={{8,0},{16,8},{24,16},{32,24},{40,32},{48,40},{56,48},{64,56},{72,6... | collective-permute-start | bytes 1572872 | tf_op jit(solution)/shard_map/ppermute | solution.py:15
  211.0 29.4 %collective-permute-start.6 = (f32[4,1,512]{2,1,0:T(1,128)S(1)}, f32[4,1,512]{2,1,0:T(1,128)S(1)}, u32[]{:S(2)}, u32[]{:S(2)}) collective-permute-start(f32[4,1,512]{2,1,0:T(1,128)S(1)} %get-tuple-element.64), channel_id=1, source_target_pairs={{0,1},{1,2},{2,3},{3,4},{4,5},{5,6},{6,7},{8,9},{9,10},{10,11},{11... | collective-permute-start | bytes 24584 | tf_op jit(solution)/shard_map/ppermute | solution.py:23
  214.6 25.8 %collective-permute-start.5 = (f32[4,1,512]{2,1,0:T(1,128)S(1)}, f32[4,1,512]{2,1,0:T(1,128)S(1)}, u32[]{:S(2)}, u32[]{:S(2)}) collective-permute-start(f32[4,1,512]{2,1,0:T(1,128)S(1)} %get-tuple-element.63), channel_id=1, source_target_pairs={{1,0},{2,1},{3,2},{4,3},{5,4},{6,5},{7,6},{9,8},{10,9},{11,10},{12... | collective-permute-start | bytes 24584 | tf_op jit(solution)/shard_map/ppermute | solution.py:26
  226.7 1.9 copy-start.10
  236.9 17.7 %collective-permute-start.8 = (f32[1024,128]{1,0:T(8,128)}, f32[1024,128]{1,0:T(8,128)}, u32[]{:S(2)}, u32[]{:S(2)}) collective-permute-start(f32[1024,128]{1,0:T(8,128)} %scatter_custom_fusion.1), channel_id=1, source_target_pairs={{0,8},{8,16},{16,24},{24,32},{32,40},{40,48},{48,56},{56,64},{64,7... | collective-permute-start | bytes 1572872 | tf_op jit(solution)/shard_map/ppermute | solution.py:15
  240.4 12.2 %copy-start.7 = (f32[1024,128]{1,0:T(8,128)S(1)}, f32[1024,128]{1,0:T(8,128)}, u32[]{:S(2)}) copy-start(f32[1024,128]{1,0:T(8,128)} %get-tuple-element.79) | copy-start | bytes 1572868
where the time goes:
time: 334 us; the launch traced here: 333 us
  blocking collectives  197 us (59%)
  other arithmetic  51.1 us (15%)
  local copies, waits for them, and re-layouts  38.5 us (12%)
  starting transfers between devices  25.6 us (8%)
  matrix products  12.4 us (4%)
  between operations  5.64 us (2%)
    psum x2, blocking collectives, squares(): return lax.psum(jnp.sum(values * values), ('sub', 'blk'))  132 us
    psum x1, blocking collectives, body(): alpha = norm_now / lax.psum(jnp.sum(direction * result), ('sub', 'blk'))  65 us
    add x2, other arithmetic, body(): result + coeff_z * (direction - next_z) + prev_z * (direction - before_z)  22.5 us
    ppermute x5, starting transfers between devices, shifted(): return lax.ppermute(array, axis, pairs)  13.6 us
    ppermute x2, starting transfers between devices, with_halo(): lax.ppermute(lax.slice_in_dim(block, block.shape[dim] - width, None, axis...  8.19 us
    dot_general x8, matrix products, mortar_jump(): jnp.einsum('kc,ac->ka', gathered, proj[kind], precision=lax.Precision.HIG...  7.9 us
    scatter x2, local copies, waits for them, and re-layouts, body(): ordered = jnp.zeros_like(back).at[partner].set(back)  7.8 us
    slice x2, local copies, waits for them, and re-layouts, body(): direction[:, :, 1:]  7.67 us
  transfers between devices with their start and end apart: 9, of which 2 were waited for; matrix products, arithmetic and copies ran while one was open for 21% of the time, Pallas kernels for 0%

commit v1 on v0

v1 whole, which is shorter than its diff:
```python
import functools

import jax
import jax.numpy as jnp
from jax import lax
from jax.experimental import pallas as pl
from jax.experimental.pallas import tpu as pltpu
from jax.sharding import PartitionSpec as P

MESH = pl.DeviceIdType.MESH
F32, BF16, I32 = jnp.float32, jnp.bfloat16, jnp.int32
CX, CY, CZ = 4, 256, 512
FB, KINDS = 128, 4
GROUPS = CZ // FB
NFB = CY * GROUPS
PAD = 8
ROWS = 32
PENALTY = 4.0


def split(x):
    high = x.astype(BF16)
    low = (x - high.astype(F32)).astype(BF16)
    return jnp.concatenate([high, low], axis=1)


def fold(x):
    total = None
    for r in range(0, x.shape[0], 8):
        for c in range(0, x.shape[1], 128):
            tile = x[r : r + 8, c : c + 128]
            total = tile if total is None else total + tile
    return total


def choose(y, kind):
    out = y[:, (KINDS - 1) * FB :]
    for t in range(KINDS - 2, -1, -1):
        out = jnp.where(kind == t, y[:, t * FB : (t + 1) * FB], out)
    return out


def project(pair, double, single, kind):
    y = jnp.dot(pair, double[...], preferred_element_type=F32)
    y = y + jnp.dot(pair[:, :FB], single[...], preferred_element_type=F32)
    return choose(y, kind)


def kernel(n_sub, n_blk, b_hbm, tx_hbm, ty_hbm, tz_hbm, st_hbm, perm_hbm, type_hbm, count_hbm, proj_hbm,
           x_ref, r_ref,
           B, TX, TY, TZ, ST, W, V,
           perm_v, type_v, count_s, meta, meta_in, PROJ,
           pt2, pt1, pp2, pp1, CB, NAT, GL, GR, GT,
           face_in, last_in, sl, sl_in, sf, psf, psf_in,
           HL, HL2, J1L, C2L, J1R, C2R, Q2,
           cur, slots,
           load_sem, small_sem, ss, rs, ar_ss, ar_rs):
    s, k = lax.axis_index("sub"), lax.axis_index("blk")
    right, left = (lax.rem(s + 1, n_sub), k), (lax.rem(s + n_sub - 1, n_sub), k)
    up, down = (s, lax.rem(k + 1, n_blk)), (s, lax.rem(k + n_blk - 1, n_blk))
    column = [(lax.rem(s + i, n_sub), k) for i in range(1, n_sub)]
    row = [(s, lax.rem(k + i, n_blk)) for i in range(1, n_blk)]

    barrier = pltpu.get_barrier_semaphore()
    for peer in [column[0], column[-1], row[0], row[-1]] + column[1:-1] + row[1:-1]:
        pl.semaphore_signal(barrier, inc=1, device_id=peer, device_id_type=MESH)

    small = [
        pltpu.make_async_copy(perm_hbm, perm_v, small_sem.at[0]),
        pltpu.make_async_copy(type_hbm, type_v, small_sem.at[1]),
        pltpu.make_async_copy(count_hbm, count_s, small_sem.at[2]),
        pltpu.make_async_copy(proj_hbm, PROJ, small_sem.at[3]),
    ]
    for c in small:
        c.start()

    def load(a, i):
        src, dst = ((b_hbm, B), (tx_hbm, TX), (ty_hbm, TY), (tz_hbm, TZ), (st_hbm, ST))[a]
        to = dst.at[i, pl.ds(PAD, CY), :] if a in (0, 2) else dst.at[i]
        return pltpu.make_async_copy(src.at[i], to, load_sem.at[a, i])

    order = [(0, 3), (0, 2), (2, 3), (3, 3), (4, 3), (1, 2), (0, 0), (0, 1), (2, 0), (3, 0), (4, 0), (1, 0),
             (2, 1), (3, 1), (4, 1), (1, 1), (2, 2), (3, 2), (4, 2)]
    for a, i in order:
        load(a, i).start()

    pl.semaphore_wait(barrier, n_sub + n_blk - 2)

    def send(src, dst, n, to):
        return pltpu.make_async_remote_copy(
            src_ref=src, dst_ref=dst, send_sem=ss.at[n], recv_sem=rs.at[n], device_id=to, device_id_type=MESH
        )

    b_up = send(b_hbm.at[:, CY - 1 : CY, :], B.at[:, PAD - 1 : PAD, :], 0, up)
    b_down = send(b_hbm.at[:, 0:1, :], B.at[:, PAD + CY : PAD + CY + 1, :], 1, down)
    ty_up = send(ty_hbm.at[:, CY - 1 : CY, :], TY.at[:, PAD - 1 : PAD, :], 2, up)
    meta_right = send(meta, meta_in, 3, right)
    first_left = send(b_hbm.at[0], face_in, 4, left)
    last_right = send(b_hbm.at[CX - 1], last_in, 5, right)
    w_up = send(W.at[:, PAD + CY - 1 : PAD + CY, :], W.at[:, PAD - 1 : PAD, :], 6, up)
    w_down = send(W.at[:, PAD : PAD + 1, :], W.at[:, PAD + CY : PAD + CY + 1, :], 7, down)
    sl_right = [send(sl.at[pl.ds(q * CY, CY)], sl_in.at[pl.ds(q * CY, CY)], 8 + q, right) for q in range(GROUPS)]
    psf_left = [send(psf.at[pl.ds(q * CY, CY)], psf_in.at[pl.ds(q * CY, CY)], 12 + q, left) for q in range(GROUPS)]

    b_up.start()
    b_down.start()
    ty_up.start()
    first_left.start()
    last_right.start()

    for c in small:
        c.wait()
    meta[0:1, :] = perm_v[0]
    meta[1:2, :] = type_v[0]
    meta[2:3, :] = jnp.full((1, NFB), count_s[0, 0], I32)
    meta[3:8, :] = jnp.zeros((5, NFB), I32)
    meta_right.start()

    for t in range(KINDS):
        for source, double, single in ((PROJ[t].T, pt2, pt1), (PROJ[t], pp2, pp1)):
            high = source.astype(BF16)
            low = (source - high.astype(F32)).astype(BF16)
            at = slice(t * FB, (t + 1) * FB)
            double[0:FB, at] = high
            double[FB : 2 * FB, at] = high
            single[:, at] = low

    lane = lax.broadcasted_iota(I32, (FB, FB), 1)
    sub_row = lax.broadcasted_iota(I32, (FB, FB), 0)

    def columns_of(m, side):
        perm = m[0:1, :]
        place = jnp.bitwise_and(perm, GROUPS - 1) * CY + lax.shift_right_logical(perm, 2)
        live = (lax.broadcasted_iota(I32, (1, NFB), 1) < m[2:3, :]).astype(I32)
        code = (place + m[1:2, :] * NFB + live * (NFB * KINDS)).astype(F32)
        for i in range(NFB // FB):
            part = jnp.broadcast_to(code[:, i * FB : (i + 1) * FB], (FB, FB))
            NAT[i * FB : (i + 1) * FB, :] = part.T
        for q in range(GROUPS):
            CB[side, q * CY : (q + 1) * CY, :] = NAT[pl.ds(q, CY, stride=GROUPS), :].astype(I32)

    def one_hot(side, G):
        def step(i, _):
            r = pl.multiple_of(i * FB, FB)
            place = jnp.bitwise_and(CB[side, pl.ds(r, FB), :], NFB - 1)
            for j in range(NFB // FB):
                G[pl.ds(r, FB), j * FB : (j + 1) * FB] = jnp.where(place == lane + j * FB, 1.0, 0.0).astype(BF16)
            return 0
        lax.fori_loop(0, NFB // FB, step, 0)

    def one_hot_back(side, G):
        for i in range(NFB // FB):
            place = jnp.bitwise_and(CB[side, i * FB : (i + 1) * FB, :], NFB - 1).astype(F32).T.astype(I32)
            def step(j, _):
                r = pl.multiple_of(j * FB, FB)
                G[pl.ds(r, FB), i * FB : (i + 1) * FB] = jnp.where(place == sub_row + r, 1.0, 0.0).astype(BF16)
                return 0
            lax.fori_loop(0, NFB // FB, step, 0)

    def kind_of(side, r):
        return jnp.bitwise_and(lax.shift_right_logical(CB[side, pl.ds(r, CY), :], 10), KINDS - 1)

    def live_of(side, r):
        return lax.shift_right_logical(CB[side, pl.ds(r, CY), :], 12).astype(F32)

    columns_of(meta, 0)
    one_hot(0, GL)

    def stencil(S, i, c):
        y = pl.multiple_of(c * ROWS, ROWS)
        here = pl.ds(y, ROWS)
        big = S[i, pl.ds(y, ROWS + 2 * PAD), :]
        mid = big[PAD : PAD + ROWS]
        after = pltpu.roll(big, ROWS + 2 * PAD - 1, 0)
        flux = TY[i, pl.ds(y, ROWS + PAD), :] * (big[: PAD + ROWS] - after[: PAD + ROWS])
        out = ST[i, here, :] * mid + (flux[PAD:] - pltpu.roll(flux, 1, 0)[PAD:])
        flux = TZ[i, here, :] * (mid - pltpu.roll(mid, CZ - 1, 1))
        out = out + (flux - pltpu.roll(flux, 1, 1))
        inner = pl.ds(pl.multiple_of(y + PAD, PAD), ROWS)
        if i < CX - 1:
            out = out + TX[i, here, :] * (mid - S[i + 1, inner, :])
        if i > 0:
            out = out - TX[i - 1, here, :] * (S[i - 1, inner, :] - mid)
        return mid, out, inner, here

    def prepare(i):
        edge = TZ[i, :, CZ - FB :]
        TZ[i, :, CZ - FB :] = jnp.where(lax.broadcasted_iota(I32, (CY, FB), 1) == FB - 1, 0.0, edge)
        TY[i, PAD + CY - 1 : PAD + CY, :] = jnp.where(k < n_blk - 1, TY[i, PAD + CY - 1 : PAD + CY, :], 0.0)
        TY[i, PAD - 1 : PAD, :] = jnp.where(k > 0, TY[i, PAD - 1 : PAD, :], 0.0)

    for a, i in order[:6]:
        load(a, i).wait()
    b_up.wait_recv()
    b_down.wait_recv()
    ty_up.wait_recv()
    prepare(3)

    def last_face(c, _):
        mid, out, inner, here = stencil(B, 3, c)
        W[3, inner, :] = out
        for q in range(GROUPS):
            sl[pl.ds(pl.multiple_of(q * CY + c * ROWS, ROWS), ROWS), :] = out[:, q * FB : (q + 1) * FB]
        return 0

    lax.fori_loop(0, CY // ROWS, last_face, 0)
    for q in (2, 3, 0, 1):
        sl_right[q].start()

    for a, i in order[6:12]:
        load(a, i).wait()
    prepare(0)

    def first_face(c, _):
        mid, out, inner, here = stencil(B, 0, c)
        W[0, inner, :] = out
        for q in range(GROUPS):
            at = pl.ds(pl.multiple_of(q * CY + c * ROWS, ROWS), ROWS)
            cols = slice(q * FB, (q + 1) * FB)
            HL[at, :] = split(mid[:, cols])
            HL2[at, :] = split(out[:, cols])
        return 0

    lax.fori_loop(0, CY // ROWS, first_face, 0)

    meta_right.wait_recv()
    columns_of(meta_in, 1)
    one_hot(1, GR)

    def gather_first(q, _):
        r = pl.multiple_of(q * CY, CY)
        at = pl.ds(r, CY)
        kind = kind_of(1, r)
        g = jnp.dot(GR[at, :], HL2[...], preferred_element_type=F32)
        psf[at, :] = project(g.astype(BF16), pt2, pt1, kind)
        g = jnp.dot(GR[at, :], HL[...], preferred_element_type=F32)
        J1R[at, :] = project(g.astype(BF16), pt2, pt1, kind)
        return 0

    lax.fori_loop(0, GROUPS, gather_first, 0)
    for q in (0, 1, 2, 3):
        psf_left[q].start()

    one_hot_back(1, GT)

    for a, i in order[12:]:
        load(a, i).wait()
    zero = jnp.zeros((8, 128), F32)
    sums = (zero, zero, zero)
    for i in (1, 2):
        prepare(i)

        def middle(c, acc, i=i):
            mid, out, inner, here = stencil(B, i, c)
            W[i, inner, :] = out
            return acc[0] + fold(mid * mid), acc[1] + fold(mid * out), acc[2] + fold(out * out)

        sums = lax.fori_loop(0, CY // ROWS, middle, sums)

    has_right = (s < n_sub - 1).astype(F32)
    has_left = (s > 0).astype(F32)
    first_left.wait_recv()
    for q in range(GROUPS):
        HL[q * CY : (q + 1) * CY, :] = split(face_in[:, q * FB : (q + 1) * FB] * has_right)

    def last_jump(q, acc):
        r = pl.multiple_of(q * CY, CY)
        at, cols = pl.ds(r, CY), pl.ds(pl.multiple_of(q * FB, FB), FB)
        kind, live = kind_of(0, r), live_of(0, r)
        g = jnp.dot(GL[at, :], HL[...], preferred_element_type=F32).astype(BF16)
        mid = B[3, pl.ds(PAD, CY), cols]
        jump = live * (mid - project(g, pt2, pt1, kind))
        w = W[3, pl.ds(PAD, CY), cols] + PENALTY * jump
        W[3, pl.ds(PAD, CY), cols] = w
        back = project(split(jump), pp2, pp1, kind)
        C2L[at, :] = w + (PENALTY * has_right) * project(split(back), pt2, pt1, kind)
        return acc[0] + fold(mid * mid), acc[1] + fold(mid * w), acc[2] + fold(w * w)

    sums = lax.fori_loop(0, GROUPS, last_jump, sums)

    last_right.wait_recv()

    def first_jump(q, _):
        r = pl.multiple_of(q * CY, CY)
        at, cols = pl.ds(r, CY), pl.ds(pl.multiple_of(q * FB, FB), FB)
        kind, live = kind_of(1, r), live_of(1, r)
        jump = has_left * live * (last_in[:, cols] - J1R[at, :])
        back = project(split(jump), pp2, pp1, kind)
        HL2[at, :] = split(back)
        C2R[at, :] = PENALTY * jump - psf[at, :] + PENALTY * project(split(back), pt2, pt1, kind)
        return 0

    lax.fori_loop(0, GROUPS, first_jump, 0)

    def first_back(q, acc):
        at, cols = pl.ds(pl.multiple_of(q * CY, CY), CY), pl.ds(pl.multiple_of(q * FB, FB), FB)
        g = jnp.dot(GT[at, :], HL2[...], preferred_element_type=F32)
        w = W[0, pl.ds(PAD, CY), cols] - PENALTY * (g[:, :FB] + g[:, FB:])
        W[0, pl.ds(PAD, CY), cols] = w
        mid = B[0, pl.ds(PAD, CY), cols]
        return acc[0] + fold(mid * mid), acc[1] + fold(mid * w), acc[2] + fold(w * w)

    sums = lax.fori_loop(0, GROUPS, first_back, sums)

    w_up.start()
    w_down.start()

    def second(c, acc):
        for i in range(CX):
            mid, out, inner, here = stencil(W, i, c)
            V[i, here, :] = out
            acc = acc + fold(mid * out)
        return acc

    wv = lax.fori_loop(1, CY // ROWS - 1, second, zero)
    w_up.wait_recv()
    w_down.wait_recv()
    wv = second(0, wv)
    wv = second(CY // ROWS - 1, wv)

    def left_second(q):
        at, cols = slice(q * CY, (q + 1) * CY), slice(q * FB, (q + 1) * FB)
        psf_left[q].wait_recv()
        jump = live_of(0, q * CY) * (C2L[at, :] - has_right * psf_in[at, :])
        V[3, :, cols] = V[3, :, cols] + PENALTY * jump
        return fold(jump * jump)

    def right_second(q):
        at = slice(q * CY, (q + 1) * CY)
        sl_right[q].wait_recv()
        jump = has_left * live_of(1, q * CY) * (sl_in[at, :] + C2R[at, :])
        Q2[...] = split(project(split(jump), pp2, pp1, kind_of(1, q * CY)))

        def back(p, _):
            rows, cols = pl.ds(pl.multiple_of(p * CY, CY), CY), pl.ds(pl.multiple_of(p * FB, FB), FB)
            g = jnp.dot(GT[rows, at], Q2[...], preferred_element_type=F32)
            V[0, :, cols] = V[0, :, cols] - PENALTY * (g[:, :FB] + g[:, FB:])
            return 0

        lax.fori_loop(0, GROUPS, back, 0)
        return fold(jump * jump)

    no_right = 1.0 - has_right
    mortar = zero
    for q in (2, 3):
        only = live_of(0, q * CY) * C2L[q * CY : (q + 1) * CY, :]
        mortar = mortar + no_right * fold(only * only)
    mortar = mortar + left_second(0) + right_second(2) + left_second(1) + right_second(3)
    wv = wv + PENALTY * mortar

    lane_row = lax.broadcasted_iota(I32, (1, 128), 1)
    packed = jnp.zeros((1, 128), F32)
    for n, part in enumerate((sums[0], sums[1], sums[2], wv)):
        packed = jnp.where(lane_row == n, jnp.sum(part), packed)
    cur[0, 0:1, :] = packed

    def spread(stage, peers):
        out = []
        for i, peer in enumerate(peers):
            c = pltpu.make_async_remote_copy(
                src_ref=cur.at[stage, 0:1], dst_ref=slots.at[stage, i : i + 1],
                send_sem=ar_ss.at[stage], recv_sem=ar_rs.at[stage], device_id=peer, device_id_type=MESH,
            )
            c.start()
        return len(peers)

    def collect(stage, count):
        arrived = slots.at[stage, 0:count]
        pltpu.make_async_copy(arrived, arrived, ar_rs.at[stage]).wait()
        return cur[stage, 0:1, :] + jnp.sum(slots[stage, 0:count, :], axis=0, keepdims=True)

    n0 = spread(0, column)
    left_second(2)
    right_second(0)
    cur[1, 0:1, :] = collect(0, n0)
    n1 = spread(1, row)
    left_second(3)
    right_second(1)
    total = collect(1, n1)

    bb, bw, ww, wv = (total[0:1, n : n + 1] for n in range(4))
    alpha = bb / bw
    rr = alpha * alpha * ww - bb
    beta = rr / bb
    curve = bw - 2.0 * alpha * ww + alpha * alpha * wv - beta * beta * bw
    alpha2 = rr / curve
    first = alpha + alpha2 * (1.0 + beta)
    cross = alpha * alpha2

    def finish(c, _):
        y = pl.multiple_of(c * ROWS, ROWS)
        here, inner = pl.ds(y, ROWS), pl.ds(pl.multiple_of(y + PAD, PAD), ROWS)
        for i in range(CX):
            b, w = B[i, inner, :], W[i, inner, :]
            x_ref[i, here, :] = first * b - cross * w
            r_ref[i, here, :] = b - first * w + cross * V[i, here, :]
        return 0

    lax.fori_loop(0, CY // ROWS, finish, 0)

    for c in [b_up, b_down, ty_up, meta_right, first_left, last_right, w_up, w_down] + sl_right + psf_left:
        c.wait_send()
    for stage, count in ((0, n0), (1, n1)):
        sent = slots.at[stage, 0:count]
        pltpu.make_async_copy(sent, sent, ar_ss.at[stage]).wait()


def body(mesh, b, tx, ty, tz, st, perm, kind, count, proj):
    n_sub, n_blk = mesh.shape["sub"], mesh.shape["blk"]
    vm = lambda *shape, dtype=F32: pltpu.VMEM(shape, dtype)
    face = (NFB, FB)
    scratch = [
        vm(CX, CY + 2 * PAD, CZ), vm(CX, CY, CZ), vm(CX, CY + PAD, CZ), vm(CX, CY, CZ), vm(CX, CY, CZ),
        vm(CX, CY + 2 * PAD, CZ), vm(CX, CY, CZ),
        vm(1, 1, NFB, dtype=I32), vm(1, 1, NFB, dtype=I32), pltpu.SMEM((1, 1), I32),
        vm(8, NFB, dtype=I32), vm(8, NFB, dtype=I32), vm(KINDS, FB, FB),
        vm(2 * FB, KINDS * FB, dtype=BF16), vm(FB, KINDS * FB, dtype=BF16),
        vm(2 * FB, KINDS * FB, dtype=BF16), vm(FB, KINDS * FB, dtype=BF16),
        vm(2, NFB, FB, dtype=I32), vm(NFB, FB),
        vm(NFB, NFB, dtype=BF16), vm(NFB, NFB, dtype=BF16), vm(NFB, NFB, dtype=BF16),
        vm(CY, CZ), vm(CY, CZ), vm(*face), vm(*face), vm(*face), vm(*face), vm(*face),
        vm(NFB, 2 * FB, dtype=BF16), vm(NFB, 2 * FB, dtype=BF16), vm(*face), vm(*face), vm(*face), vm(*face),
        vm(CY, 2 * FB, dtype=BF16),
        vm(2, 8, 128), vm(2, 16, 128),
        pltpu.SemaphoreType.DMA((5, CX)), pltpu.SemaphoreType.DMA((4,)),
        pltpu.SemaphoreType.DMA((16,)), pltpu.SemaphoreType.DMA((16,)),
        pltpu.SemaphoreType.DMA((2,)), pltpu.SemaphoreType.DMA((2,)),
    ]
    out = jax.ShapeDtypeStruct((CX, CY, CZ), F32)
    return tuple(pl.pallas_call(
        functools.partial(kernel, n_sub, n_blk),
        out_shape=(out, out),
        in_specs=[pl.BlockSpec(memory_space=pl.ANY)] * 9,
        out_specs=(pl.BlockSpec(memory_space=pltpu.VMEM),) * 2,
        scratch_shapes=scratch,
        compiler_params=pltpu.CompilerParams(
            collective_id=0, has_side_effects=True, vmem_limit_bytes=44 * 1024 * 1024
        ),
        name="darcy_cg",
    )(b, tx, ty, tz, st, perm, kind, count, proj))


def solution(mesh):
    cells = P("sub", "blk", None)
    return jax.shard_map(
        functools.partial(body, mesh), mesh=mesh,
        in_specs=(cells,) * 7 + (P("sub", "blk"), P()), out_specs=(cells, cells), check_vma=False,
    )
```

time: 334 us -> 65.8 us (0.20)
  blocking collectives: 197 us -> 0 us
  Pallas kernels: 0 us -> 56.1 us
  other arithmetic: 51.1 us -> 0 us
  local copies, waits for them, and re-layouts: 38.5 us -> 8.14 us
  starting transfers between devices: 25.6 us -> 0 us
  matrix products: 12.4 us -> 0 us
  between operations: 5.64 us -> 1.3 us
    psum x3 -> x0, blocking collectives: 197 us -> none  [the longest x2 132 us: squares(): return lax.psum(jnp.sum(values * values), ('sub', 'blk'))]
    pallas_call x0 -> x1, Pallas kernels: none -> 56.1 us  [body(): pl.pallas_call(functools.partial(kernel, n_sub, n_blk), out_shape=(out, o...]
    ppermute x9 -> x0, starting transfers between devices: 25.6 us -> none  [the longest x5 13.6 us: shifted(): return lax.ppermute(array, axis, pairs)]
    add x3 -> x0, other arithmetic: 24.6 us -> none  [the longest x2 22.5 us: body(): result + coeff_z * (direction - next_z) + prev_z * (direction - before_z)]
    slice x10 -> x0, local copies, waits for them, and re-layouts: 15.4 us -> none  [the longest x2 7.67 us: body(): direction[:, :, 1:]]
    dot_general x16 -> x0, matrix products: 12.4 us -> none  [the longest x8 7.9 us: mortar_jump(): jnp.einsum('kc,ac->ka', gathered, proj[kind], precision=lax.Precision.HIG...]
    reduce_sum x3 -> x0, other arithmetic: 8.83 us -> none  [the longest x2 6.09 us: body(): alpha = norm_now / lax.psum(jnp.sum(direction * result), ('sub', 'blk'))]
    scatter x2 -> x0, local copies, waits for them, and re-layouts: 7.8 us -> none  [body(): ordered = jnp.zeros_like(back).at[partner].set(back)]
  transfers between devices with their start and end apart: 9 -> 0, of which waited for: 2 -> 0; matrix products, arithmetic and copies ran while one was open for 21% -> 0% of each run, Pallas kernels for 0% -> 0%
where the time goes in v1:
time: 65.8 us; the launch traced here: 65.6 us
  Pallas kernels  56.1 us (85%)
  local copies, waits for them, and re-layouts  8.14 us (12%)
  between operations  1.3 us (2%)
    pallas_call x1, Pallas kernels, body(): pl.pallas_call(functools.partial(kernel, n_sub, n_blk), out_shape=(out, o...  56.1 us
    unnamed x12, local copies, waits for them, and re-layouts  8.14 us

profile of v1, /device:TPU:1, one launch (start us, length us, event | category | flops | bytes accessed | tf_op | source)
XLA Modules:
  0.0 65.6 jit_solution(10030116557767967882)
XLA Ops:
  1.3 0.0 copy-start
  1.3 1.6 %copy-done = f32[4,256,512]{2,1,0:T(8,128)S(1)} copy-done((f32[4,256,512]{2,1,0:T(8,128)S(1)}, f32[4,256,512]{2,1,0:T(8,128)}, u32[]{:S(2)}) %copy-start) | copy-done | bytes 2097176
  2.9 0.0 copy-start.1
  2.9 1.6 %copy-done.1 = f32[4,256,512]{2,1,0:T(8,128)S(1)} copy-done((f32[4,256,512]{2,1,0:T(8,128)S(1)}, f32[4,256,512]{2,1,0:T(8,128)}, u32[]{:S(2)}) %copy-start.1) | copy-done | bytes 2097176
  4.5 0.0 copy-start.2
  4.5 0.9 %copy-done.2 = f32[4,128,128]{2,1,0:T(8,128)S(1)} copy-done((f32[4,128,128]{2,1,0:T(8,128)S(1)}, f32[4,128,128]{2,1,0:T(8,128)}, u32[]{:S(2)}) %copy-start.2) | copy-done | bytes 262168
  5.4 0.0 copy-start.3
  5.4 0.7 %copy-done.3 = s32[1,1,1024]{2,1,0:T(1,128)S(1)} copy-done((s32[1,1,1024]{2,1,0:T(1,128)S(1)}, s32[1,1,1024]{2,1,0:T(1,128)}, u32[]{:S(2)}) %copy-start.3) | copy-done | bytes 4120
  6.1 0.0 copy-start.4
  6.1 0.7 %copy-done.4 = s32[1,1,1024]{2,1,0:T(1,128)S(1)} copy-done((s32[1,1,1024]{2,1,0:T(1,128)S(1)}, s32[1,1,1024]{2,1,0:T(1,128)}, u32[]{:S(2)}) %copy-start.4) | copy-done | bytes 4120
  6.8 56.1 %darcy_cg.1 = (f32[4,256,512]{2,1,0:T(8,128)S(1)}, f32[4,256,512]{2,1,0:T(8,128)S(1)}) custom-call(f32[4,256,512]{2,1,0:T(8,128)S(1)} %copy-done, f32[4,256,512]{2,1,0:T(8,128)S(1)} %copy-done.1, f32[4,256,512]{2,1,0:T(8,128)} %ty_hbm.1, f32[4,256,512]{2,1,0:T(8,128)} %tz_hbm.1, f32[4,256,512]{2,1,0:T(8,128)} %st_hbm.1, s32[1,1,1024]{2,1,0:T(1,128)S(1)} %copy-done.3, ...), custom_call_target="tpu_custom_call" | custom-call | tf_op jit(solution)/shard_map/darcy_cg/pallas_call | solution.py:430
  62.9 1.3 %copy.14 = f32[4,256,512]{2,1,0:T(8,128)} copy(f32[4,256,512]{2,1,0:T(8,128)S(1)} %get-tuple-element.4) | data formatting | bytes 4194304
  64.2 1.3 %copy.15 = f32[4,256,512]{2,1,0:T(8,128)} copy(f32[4,256,512]{2,1,0:T(8,128)S(1)} %get-tuple-element.5) | data formatting | bytes 4194304
Async XLA Ops:
  1.3 1.6 %copy-start = (f32[4,256,512]{2,1,0:T(8,128)S(1)}, f32[4,256,512]{2,1,0:T(8,128)}, u32[]{:S(2)}) copy-start(f32[4,256,512]{2,1,0:T(8,128)} %b_hbm.1) | copy-start | bytes 6291460
  2.9 1.6 %copy-start.1 = (f32[4,256,512]{2,1,0:T(8,128)S(1)}, f32[4,256,512]{2,1,0:T(8,128)}, u32[]{:S(2)}) copy-start(f32[4,256,512]{2,1,0:T(8,128)} %tx_hbm.1) | copy-start | bytes 6291460
  4.5 0.9 %copy-start.2 = (f32[4,128,128]{2,1,0:T(8,128)S(1)}, f32[4,128,128]{2,1,0:T(8,128)}, u32[]{:S(2)}) copy-start(f32[4,128,128]{2,1,0:T(8,128)} %proj_hbm.1) | copy-start | bytes 786436
  5.4 0.7 %copy-start.3 = (s32[1,1,1024]{2,1,0:T(1,128)S(1)}, s32[1,1,1024]{2,1,0:T(1,128)}, u32[]{:S(2)}) copy-start(s32[1,1,1024]{2,1,0:T(1,128)} %perm_hbm.1) | copy-start | bytes 12292
  6.1 0.7 %copy-start.4 = (s32[1,1,1024]{2,1,0:T(1,128)S(1)}, s32[1,1,1024]{2,1,0:T(1,128)}, u32[]{:S(2)}) copy-start(s32[1,1,1024]{2,1,0:T(1,128)} %type_hbm.1) | copy-start | bytes 12292

commit v2 on v1

v2 whole, which is shorter than its diff:
```python
import functools

import jax
import jax.numpy as jnp
from jax import lax
from jax.experimental import pallas as pl
from jax.experimental.pallas import tpu as pltpu
from jax.sharding import PartitionSpec as P

MESH = pl.DeviceIdType.MESH
F32, BF16, I32 = jnp.float32, jnp.bfloat16, jnp.int32
CX, CY, CZ = 4, 256, 512
FB, KINDS = 128, 4
GROUPS = CZ // FB
NFB = CY * GROUPS
PAD = 8
ROWS = 128
BAND = CY // GROUPS
PENALTY = 4.0


def split(x):
    high = x.astype(BF16)
    low = (x - high.astype(F32)).astype(BF16)
    return jnp.concatenate([high, low], axis=1)


def fold(x):
    total = None
    for r in range(0, x.shape[0], 8):
        for c in range(0, x.shape[1], 128):
            tile = x[r : r + 8, c : c + 128]
            total = tile if total is None else total + tile
    return total


def kernel(n_sub, n_blk, b_hbm, tx_hbm, ty_hbm, tz_hbm, st_hbm, perm_hbm, type_hbm, proj_hbm, count_s,
           B, W, V, scalars,
           TX, TY, TZ, ST,
           perm_v, type_v, meta, meta_in, PROJ,
           wpt, wpp, wm, CB, LOW, NAT, GL, GR, GT,
           face_in, last_in, sl, sl_in, psf, psf_in,
           HL, HL2, HJ, ACC, C2L, J1R, C2R,
           edges, cur, slots,
           load_sem, small_sem, ss, rs, ar_ss, ar_rs):
    s, k = lax.axis_index("sub"), lax.axis_index("blk")
    right, left = (lax.rem(s + 1, n_sub), k), (lax.rem(s + n_sub - 1, n_sub), k)
    up, down = (s, lax.rem(k + 1, n_blk)), (s, lax.rem(k + n_blk - 1, n_blk))
    column = [(lax.rem(s + i, n_sub), k) for i in (10, 6, 14, 9, 11, 2, 5, 7, 13, 8, 3, 4, 12, 1, 15)]
    row = [(s, lax.rem(k + i, n_blk)) for i in (4, 3, 5, 2, 6, 1, 7)]
    near = [column[-2], column[-1], row[-2], row[-1]]
    has_left, has_right, has_down, has_up = s > 0, s < n_sub - 1, k > 0, k < n_blk - 1

    barrier = pltpu.get_barrier_semaphore()
    for peer in near + column[:-2] + row[:-2]:
        pl.semaphore_signal(barrier, inc=1, device_id=peer, device_id_type=MESH)

    small = [
        pltpu.make_async_copy(perm_hbm, perm_v, small_sem.at[0]),
        pltpu.make_async_copy(type_hbm, type_v, small_sem.at[1]),
        pltpu.make_async_copy(proj_hbm, PROJ, small_sem.at[2]),
    ]
    for c in small:
        c.start()

    def load(a, i):
        src, dst = ((b_hbm, B), (tx_hbm, TX), (ty_hbm, TY), (tz_hbm, TZ), (st_hbm, ST))[a]
        to = dst.at[i, pl.ds(PAD, CY), :] if a in (0, 2) else dst.at[i]
        return pltpu.make_async_copy(src.at[i], to, load_sem.at[a, i])

    order = [(0, 3), (0, 2), (2, 3), (3, 3), (4, 3), (1, 2), (0, 0), (0, 1), (2, 0), (3, 0), (4, 0), (1, 0),
             (2, 1), (3, 1), (4, 1), (1, 1), (2, 2), (3, 2), (4, 2)]
    loads = {key: load(*key) for key in order}
    for key in order[:6]:
        loads[key].start()

    @pl.when(s == 0)
    def _():
        meta_in[...] = jnp.zeros_like(meta_in)
        last_in[...] = jnp.zeros_like(last_in)
        sl_in[...] = jnp.zeros_like(sl_in)

    @pl.when(s == n_sub - 1)
    def _():
        face_in[...] = jnp.zeros_like(face_in)
        psf_in[...] = jnp.zeros_like(psf_in)

    @pl.when(k == 0)
    def _():
        for n in (0, 2, 3):
            edges[n] = jnp.zeros((CX, 8, CZ), F32)

    @pl.when(k == n_blk - 1)
    def _():
        for n in (1, 4):
            edges[n] = jnp.zeros((CX, 8, CZ), F32)

    for c in small:
        c.wait()
    meta[0:1, :] = perm_v[0]
    meta[1:2, :] = type_v[0]
    meta[2:3, :] = jnp.full((1, NFB), count_s[0, 0], I32)
    meta[3:8, :] = jnp.zeros((5, NFB), I32)

    pl.semaphore_wait(barrier, n_sub + n_blk - 2)

    class Send:
        def __init__(self, src, dst, n, to, sends, receives):
            self.sends, self.receives = sends, receives
            self.copy = pltpu.make_async_remote_copy(
                src_ref=src, dst_ref=dst, send_sem=ss.at[n], recv_sem=rs.at[n], device_id=to, device_id_type=MESH
            )

        def start(self):
            pl.when(self.sends)(self.copy.start)

        def wait_send(self):
            pl.when(self.sends)(self.copy.wait_send)

        def wait_recv(self):
            pl.when(self.receives)(self.copy.wait_recv)

    to_up, to_down = (up, has_up, has_down), (down, has_down, has_up)
    to_right, to_left = (right, has_right, has_left), (left, has_left, has_right)
    b_up = Send(b_hbm.at[:, CY - 1 : CY, :], edges.at[0, :, 0:1, :], 0, *to_up)
    b_down = Send(b_hbm.at[:, 0:1, :], edges.at[1, :, 0:1, :], 1, *to_down)
    ty_up = Send(ty_hbm.at[:, CY - 1 : CY, :], edges.at[2, :, 0:1, :], 2, *to_up)
    meta_right = Send(meta, meta_in, 3, *to_right)
    w_up = Send(W.at[:, PAD + CY - 1 : PAD + CY, :], edges.at[3, :, 0:1, :], 4, *to_up)
    w_down = Send(W.at[:, PAD : PAD + 1, :], edges.at[4, :, 0:1, :], 5, *to_down)
    quarter = [pl.ds(q * CY, CY) for q in range(GROUPS)]
    sl_right = [Send(sl.at[quarter[q]], sl_in.at[quarter[q]], 6 + q, *to_right) for q in range(GROUPS)]
    psf_left = [Send(psf.at[quarter[q]], psf_in.at[quarter[q]], 10 + q, *to_left) for q in range(GROUPS)]
    parts = [pl.ds(0, CY - BAND), pl.ds(CY - BAND, BAND)]
    first_left = [Send(b_hbm.at[0, p], face_in.at[p], 14 + n, *to_left) for n, p in enumerate(parts)]
    last_right = [Send(b_hbm.at[CX - 1, p], last_in.at[p], 16 + n, *to_right) for n, p in enumerate(parts)]

    b_up.start()
    b_down.start()
    ty_up.start()
    meta_right.start()
    for n in range(2):
        first_left[n].start()
        last_right[n].start()
    for key in order[6:]:
        loads[key].start()

    def place_matrix(target, t, matrix):
        high = matrix.astype(BF16)
        low = (matrix - high.astype(F32)).astype(BF16)
        at, base = slice((t % 2) * FB, (t % 2 + 1) * FB), t // 2
        target[base * 2 * FB : (base * 2 + 1) * FB, at] = high
        target[(base * 2 + 1) * FB : (base * 2 + 2) * FB, at] = high
        target[(4 + base) * FB : (5 + base) * FB, at] = low

    for t in range(KINDS):
        matrix = PROJ[t]
        turned = matrix.T
        place_matrix(wpt, t, turned)
        place_matrix(wpp, t, matrix)
        place_matrix(wm, t, jnp.dot(matrix, turned, precision=lax.Precision.HIGHEST, preferred_element_type=F32))

    lane = lax.broadcasted_iota(I32, (FB, FB), 1)
    sub_row = lax.broadcasted_iota(I32, (FB, FB), 0)

    def columns_of(m, side):
        perm = m[0:1, :]
        y = lax.shift_right_logical(perm, 2)
        place = (lax.shift_right_logical(y, 6) * CY + jnp.bitwise_and(perm, GROUPS - 1) * BAND
                 + jnp.bitwise_and(y, BAND - 1))
        live = (lax.broadcasted_iota(I32, (1, NFB), 1) < m[2:3, :]).astype(I32)
        code = (place + m[1:2, :] * NFB + live * (NFB * KINDS)).astype(F32)
        for i in range(NFB // FB):
            part = jnp.broadcast_to(code[:, i * FB : (i + 1) * FB], (FB, FB))
            NAT[i * FB : (i + 1) * FB, :] = part.T
        for n in range(GROUPS * GROUPS):
            at = slice(n * BAND, (n + 1) * BAND)
            c = NAT[pl.ds((n // GROUPS) * CY + n % GROUPS, BAND, stride=GROUPS), :].astype(I32)
            CB[side, at, :] = c
            LOW[side, at, :] = jnp.where(jnp.bitwise_and(c, 2 * NFB) == 0, 1.0, 0.0).astype(BF16)

    def one_hot(side, G):
        def step(i, _):
            r = pl.multiple_of(i * FB, FB)
            place = jnp.bitwise_and(CB[side, pl.ds(r, FB), :], NFB - 1)
            for j in range(NFB // FB):
                G[pl.ds(r, FB), j * FB : (j + 1) * FB] = jnp.where(place == lane + j * FB, 1.0, 0.0).astype(BF16)
            return 0
        lax.fori_loop(0, NFB // FB, step, 0)

    def one_hot_back(side, G):
        for i in range(NFB // FB):
            place = jnp.bitwise_and(CB[side, i * FB : (i + 1) * FB, :], NFB - 1).astype(F32).T.astype(I32)
            def step(j, _):
                r = pl.multiple_of(j * FB, FB)
                G[pl.ds(r, FB), i * FB : (i + 1) * FB] = jnp.where(place == sub_row + r, 1.0, 0.0).astype(BF16)
                return 0
            lax.fori_loop(0, NFB // FB, step, 0)

    def live_of(side, at):
        return lax.shift_right_logical(CB[side, at, :], 12).astype(F32)

    def pieces(quarters):
        for c in quarters:
            for q in range(GROUPS):
                n = c * GROUPS + q
                yield (slice(n * BAND, (n + 1) * BAND), slice(c * BAND, (c + 1) * BAND), slice(q * FB, (q + 1) * FB),
                       slice(PAD + c * BAND, PAD + (c + 1) * BAND))

    def project(pair, target, side, at=slice(0, NFB)):
        low_kind = LOW[side, at, :]
        high_kind = 1.0 - low_kind
        high, low = pair[:, :FB], pair[:, FB:]
        ha, hb = high * low_kind, high * high_kind
        x = jnp.concatenate([ha, low * low_kind, hb, low * high_kind, ha, hb], axis=1)
        y = jnp.dot(x, target[...], preferred_element_type=F32)
        odd = jnp.bitwise_and(CB[side, at, :], NFB) != 0
        return jnp.where(odd, y[:, FB:], y[:, :FB])

    columns_of(meta, 0)
    one_hot(0, GL)

    def stencil(S, i, c):
        y = pl.multiple_of(c * ROWS, ROWS)
        here, inner = pl.ds(y, ROWS), pl.ds(pl.multiple_of(y + PAD, PAD), ROWS)
        big = S[i, pl.ds(y, ROWS + 2 * PAD), :]
        mid = big[PAD : PAD + ROWS]
        after = pltpu.roll(big, ROWS + 2 * PAD - 1, 0)
        flux = TY[i, pl.ds(y, ROWS + PAD), :] * (big[: PAD + ROWS] - after[: PAD + ROWS])
        out = ST[i, here, :] * mid + (flux[PAD:] - pltpu.roll(flux, 1, 0)[PAD:])
        flux = TZ[i, here, :] * (mid - pltpu.roll(mid, CZ - 1, 1))
        out = out + (flux - pltpu.roll(flux, 1, 1))
        if i < CX - 1:
            out = out + TX[i, here, :] * (mid - S[i + 1, inner, :])
        if i > 0:
            out = out - TX[i - 1, here, :] * (S[i - 1, inner, :] - mid)
        return mid, out, inner, here

    def energy(i, along_x):
        W[i, PAD + CY : PAD + CY + 1, :] = W[i, PAD + CY - 1 : PAD + CY, :]

        def step(c, acc):
            y = pl.multiple_of(c * ROWS, ROWS)
            here, inner = pl.ds(y, ROWS), pl.ds(pl.multiple_of(y + PAD, PAD), ROWS)
            big = W[i, pl.ds(pl.multiple_of(y + PAD, PAD), ROWS + PAD), :]
            mid = big[:ROWS]
            d = mid - pltpu.roll(big, ROWS + PAD - 1, 0)[:ROWS]
            e = ST[i, here, :] * mid * mid + TY[i, inner, :] * d * d
            d = mid - pltpu.roll(mid, CZ - 1, 1)
            e = e + TZ[i, here, :] * d * d
            if along_x:
                d = mid - W[i + 1, inner, :]
                e = e + TX[i, here, :] * d * d
            if i == CX - 1:
                d = W[i - 1, inner, :] - mid
                e = e + TX[i - 1, here, :] * d * d
            return acc + fold(e)

        return lambda acc: lax.fori_loop(0, CY // ROWS, step, acc)

    def prepare(i):
        edge = TZ[i, :, CZ - FB :]
        TZ[i, :, CZ - FB :] = jnp.where(lax.broadcasted_iota(I32, (CY, FB), 1) == FB - 1, 0.0, edge)
        TY[i, PAD + CY - 1 : PAD + CY, :] = jnp.where(has_up, TY[i, PAD + CY - 1 : PAD + CY, :], 0.0)
        TY[i, PAD - 1 : PAD, :] = edges[2, i, 0:1, :]
        B[i, PAD - 1 : PAD, :] = edges[0, i, 0:1, :]
        B[i, PAD + CY : PAD + CY + 1, :] = edges[1, i, 0:1, :]

    for a, i in order[:6]:
        loads[a, i].wait()
    b_up.wait_recv()
    b_down.wait_recv()
    ty_up.wait_recv()
    prepare(3)

    def last_face(c, _):
        mid, out, inner, here = stencil(B, 3, c)
        W[3, inner, :] = out
        for n in range(ROWS // BAND * GROUPS):
            h, q = divmod(n, GROUPS)
            at = pl.ds(pl.multiple_of(c * (ROWS * GROUPS) + n * BAND, BAND), BAND)
            sl[at, :] = out[h * BAND : (h + 1) * BAND, q * FB : (q + 1) * FB]
        return 0

    lax.fori_loop(0, CY // ROWS, last_face, 0)
    for q in (2, 3, 0, 1):
        sl_right[q].start()

    for a, i in order[6:12]:
        loads[a, i].wait()
    prepare(0)

    def first_face(c, _):
        mid, out, inner, here = stencil(B, 0, c)
        W[0, inner, :] = out
        for n in range(ROWS // BAND * GROUPS):
            h, q = divmod(n, GROUPS)
            at = pl.ds(pl.multiple_of(c * (ROWS * GROUPS) + n * BAND, BAND), BAND)
            ys, cols = slice(h * BAND, (h + 1) * BAND), slice(q * FB, (q + 1) * FB)
            HL[at, :] = split(mid[ys, cols])
            HL2[at, :] = split(out[ys, cols])
        return 0

    lax.fori_loop(0, CY // ROWS, first_face, 0)

    meta_right.wait_recv()
    columns_of(meta_in, 1)
    one_hot(1, GR)
    g = jnp.dot(GR[...], HL2[...], preferred_element_type=F32).astype(BF16)
    psf[...] = project(g, wpt, 1)
    for q in range(GROUPS):
        psf_left[q].start()
    g = jnp.dot(GR[...], HL[...], preferred_element_type=F32).astype(BF16)
    J1R[...] = project(g, wpt, 1)

    one_hot_back(1, GT)

    for a, i in order[12:]:
        loads[a, i].wait()
    zero = jnp.zeros((8, 128), F32)
    sums = (zero, zero, zero)
    for i in (1, 2):
        prepare(i)

        def middle(c, acc, i=i):
            mid, out, inner, here = stencil(B, i, c)
            W[i, inner, :] = out
            return acc[0] + fold(mid * mid), acc[1] + fold(mid * out), acc[2] + fold(out * out)

        sums = lax.fori_loop(0, CY // ROWS, middle, sums)
    wv = energy(1, True)(zero)
    wv = energy(2, False)(wv)

    right_one, left_one = has_right.astype(F32), has_left.astype(F32)
    most, rest = slice(0, NFB - CY), slice(NFB - CY, NFB)

    def gather_right(quarters, at):
        for rows, ys, cols, _ in pieces(quarters):
            HL[rows, :] = split(face_in[ys, cols])
        return jnp.dot(GL[:, at], HL[at, :], preferred_element_type=F32)

    def jumps_left(quarters, at):
        for rows, ys, cols, _ in pieces(quarters):
            jump = left_one * live_of(1, rows) * (last_in[ys, cols] - J1R[rows, :])
            HJ[rows, :] = split(jump)
            C2R[rows, :] = PENALTY * jump - psf[rows, :]
        HL2[at, :] = split(project(HJ[at, :], wpp, 1, at))
        return jnp.dot(GT[:, at], HL2[at, :], preferred_element_type=F32)

    first_left[0].wait_recv()
    last_right[0].wait_recv()
    ACC[...] = gather_right((0, 1, 2), most)
    g = jumps_left((0, 1, 2), most)
    for at, _, cols, ys in pieces(range(GROUPS)):
        W[0, ys, cols] = W[0, ys, cols] - PENALTY * (g[at, :FB] + g[at, FB:])
    first_left[1].wait_recv()
    last_right[1].wait_recv()
    g = jumps_left((3,), rest)
    for at, _, cols, ys in pieces(range(GROUPS)):
        w = W[0, ys, cols] - PENALTY * (g[at, :FB] + g[at, FB:])
        W[0, ys, cols] = w
        mid = B[0, ys, cols]
        sums = sums[0] + fold(mid * mid), sums[1] + fold(mid * w), sums[2] + fold(w * w)
    g = ACC[...] + gather_right((3,), rest)
    projected = project(g.astype(BF16), wpt, 0)
    for at, _, cols, ys in pieces(range(GROUPS)):
        mid = B[3, ys, cols]
        jump = live_of(0, at) * (mid - projected[at])
        w = W[3, ys, cols] + PENALTY * jump
        W[3, ys, cols] = w
        HL[at, :] = split(jump)
        C2L[at, :] = w
        sums = sums[0] + fold(mid * mid), sums[1] + fold(mid * w), sums[2] + fold(w * w)

    w_up.start()
    w_down.start()

    C2L[...] = C2L[...] + (PENALTY * right_one) * project(HL[...], wm, 0)
    C2R[...] = C2R[...] + PENALTY * project(HJ[...], wm, 1)
    wv = energy(0, True)(wv)
    wv = energy(3, False)(wv)

    def left_jump(q, wait=True):
        at = slice(q * CY, (q + 1) * CY)
        if wait:
            psf_left[q].wait_recv()
        return live_of(0, at) * (C2L[at, :] - psf_in[at, :])

    def right_jump(q):
        at = slice(q * CY, (q + 1) * CY)
        sl_right[q].wait_recv()
        return left_one * live_of(1, at) * (sl_in[at, :] + C2R[at, :])

    def add_left(q, jump):
        for at, ys, cols, _ in pieces((q,)):
            V[3, ys, cols] = V[3, ys, cols] + PENALTY * jump[at.start - q * CY : at.stop - q * CY]

    def add_right(pair, at):
        back = split(project(pair, wpp, 1, at))
        g = jnp.dot(GT[:, at], back, preferred_element_type=F32)
        for rows, ys, cols, _ in pieces(range(GROUPS)):
            V[0, ys, cols] = V[0, ys, cols] - PENALTY * (g[rows, :FB] + g[rows, FB:])

    no_right = 1.0 - right_one
    mortar = zero
    for q in (2, 3):
        at = slice(q * CY, (q + 1) * CY)
        only = live_of(0, at) * C2L[at, :]
        mortar = mortar + no_right * fold(only * only)
    for q in (0, 1):
        jump = left_jump(q)
        mortar = mortar + fold(jump * jump)
    for q in (2, 3):
        jump = right_jump(q)
        HJ[q * CY : (q + 1) * CY, :] = split(jump)
        mortar = mortar + fold(jump * jump)
    wv = wv + PENALTY * mortar

    w_up.wait_recv()
    w_down.wait_recv()
    across = jnp.zeros((1, CZ), F32)
    for i in range(CX):
        d = W[i, PAD + CY - 1 : PAD + CY, :] - edges[4, i, 0:1, :]
        across = across + TY[i, PAD + CY - 1 : PAD + CY, :] * d * d
        W[i, PAD - 1 : PAD, :] = edges[3, i, 0:1, :]
        W[i, PAD + CY : PAD + CY + 1, :] = edges[4, i, 0:1, :]

    lane_row = lax.broadcasted_iota(I32, (1, 128), 1)
    packed = jnp.zeros((1, 128), F32)
    for n, part in enumerate((sums[0], sums[1], sums[2])):
        packed = jnp.where(lane_row == n, jnp.sum(part), packed)
    packed = jnp.where(lane_row == 3, jnp.sum(wv) + jnp.sum(across), packed)
    cur[0, 0:1, :] = packed

    def spread(stage, peers):
        for i, peer in enumerate(peers):
            pltpu.make_async_remote_copy(
                src_ref=cur.at[stage, 0:1], dst_ref=slots.at[stage, i : i + 1],
                send_sem=ar_ss.at[stage], recv_sem=ar_rs.at[stage], device_id=peer, device_id_type=MESH,
            ).start()
        return len(peers)

    def collect(stage, count):
        arrived = slots.at[stage, 0:count]
        pltpu.make_async_copy(arrived, arrived, ar_rs.at[stage]).wait()
        return cur[stage, 0:1, :] + jnp.sum(slots[stage, 0:count, :], axis=0, keepdims=True)

    n0 = spread(0, column)

    for i in (3, 0, 1, 2):
        def second(c, _, i=i):
            mid, out, inner, here = stencil(W, i, c)
            V[i, here, :] = out
            return 0
        lax.fori_loop(0, CY // ROWS, second, 0)
    for q in (0, 1):
        add_left(q, left_jump(q, wait=False))
    add_right(HJ[2 * CY :, :], slice(2 * CY, 4 * CY))

    cur[1, 0:1, :] = collect(0, n0)
    n1 = spread(1, row)

    for q in (2, 3):
        add_left(q, left_jump(q))
    for q in (0, 1):
        add_right(split(right_jump(q)), slice(q * CY, (q + 1) * CY))

    total = collect(1, n1)
    bb, bw, ww, wv = (total[0:1, n : n + 1] for n in range(4))
    alpha = bb / bw
    rr = alpha * alpha * ww - bb
    beta = rr / bb
    curve = bw - 2.0 * alpha * ww + alpha * alpha * wv - beta * beta * bw
    alpha2 = rr / curve
    scalars[0:8, :] = jnp.broadcast_to(alpha + alpha2 * (1.0 + beta), (8, 128))
    scalars[8:16, :] = jnp.broadcast_to(alpha * alpha2, (8, 128))

    for c in [b_up, b_down, ty_up, meta_right, w_up, w_down] + first_left + last_right + sl_right + psf_left:
        c.wait_send()
    for stage, count in ((0, n0), (1, n1)):
        sent = slots.at[stage, 0:count]
        pltpu.make_async_copy(sent, sent, ar_ss.at[stage]).wait()


def finish_kernel(B, W, V, scalars, x_hbm, r_hbm, x_v, r_v, sem):
    first, cross = scalars[0:1, 0:1], scalars[8:9, 0:1]
    out = []
    for i in range(CX):
        for h in range(2):
            n = 2 * i + h
            here, inner = pl.ds(h * ROWS, ROWS), pl.ds(PAD + h * ROWS, ROWS)
            b, w = B[i, inner, :], W[i, inner, :]
            x_v[i, here, :] = first * b - cross * w
            out.append(pltpu.make_async_copy(x_v.at[i, here], x_hbm.at[i, here], sem.at[0, n]))
            out[-1].start()
            r_v[i, here, :] = b - first * w + cross * V[i, here, :]
            out.append(pltpu.make_async_copy(r_v.at[i, here], r_hbm.at[i, here], sem.at[1, n]))
            out[-1].start()
    for c in out:
        c.wait()


def body(mesh, b, tx, ty, tz, st, perm, kind, count, proj):
    n_sub, n_blk = mesh.shape["sub"], mesh.shape["blk"]
    vm = lambda *shape, dtype=F32: pltpu.VMEM(shape, dtype)
    face, block, padded = (NFB, FB), (CX, CY, CZ), (CX, CY + 2 * PAD, CZ)
    scratch = [
        vm(*block), vm(CX, CY + PAD, CZ), vm(*block), vm(*block),
        vm(1, 1, NFB, dtype=I32), vm(1, 1, NFB, dtype=I32),
        vm(8, NFB, dtype=I32), vm(8, NFB, dtype=I32), vm(KINDS, FB, FB),
        vm(6 * FB, 2 * FB, dtype=BF16), vm(6 * FB, 2 * FB, dtype=BF16), vm(6 * FB, 2 * FB, dtype=BF16),
        vm(2, NFB, FB, dtype=I32), vm(2, NFB, FB, dtype=BF16), vm(*face),
        vm(NFB, NFB, dtype=BF16), vm(NFB, NFB, dtype=BF16), vm(NFB, NFB, dtype=BF16),
        vm(CY, CZ), vm(CY, CZ), vm(*face), vm(*face), vm(*face), vm(*face),
        vm(NFB, 2 * FB, dtype=BF16), vm(NFB, 2 * FB, dtype=BF16), vm(NFB, 2 * FB, dtype=BF16), vm(NFB, 2 * FB),
        vm(*face), vm(*face), vm(*face),
        vm(5, CX, 8, CZ), vm(2, 8, 128), vm(2, 16, 128),
        pltpu.SemaphoreType.DMA((5, CX)), pltpu.SemaphoreType.DMA((3,)),
        pltpu.SemaphoreType.DMA((18,)), pltpu.SemaphoreType.DMA((18,)),
        pltpu.SemaphoreType.DMA((2,)), pltpu.SemaphoreType.DMA((2,)),
    ]
    like = lambda *shape: jax.ShapeDtypeStruct(shape, F32)
    in_vmem, in_hbm = pl.BlockSpec(memory_space=pltpu.VMEM), pl.BlockSpec(memory_space=pltpu.HBM)
    args = [pltpu.with_memory_space_constraint(a, pltpu.HBM) for a in (b, tx, ty, tz, st, perm, kind, proj)]
    state = pl.pallas_call(
        functools.partial(kernel, n_sub, n_blk),
        out_shape=(vm(*padded), vm(*padded), vm(*block), vm(16, 128)),
        in_specs=[in_hbm] * 8 + [pl.BlockSpec(memory_space=pltpu.SMEM)],
        out_specs=(in_vmem,) * 4,
        scratch_shapes=scratch,
        compiler_params=pltpu.CompilerParams(
            collective_id=0, has_side_effects=True, vmem_limit_bytes=48 * 1024 * 1024
        ),
        name="darcy_cg",
    )(*args, count)
    return tuple(pl.pallas_call(
        finish_kernel,
        out_shape=(like(*block), like(*block)),
        in_specs=[in_vmem] * 4,
        out_specs=(in_hbm,) * 2,
        scratch_shapes=[vm(*block), vm(*block), pltpu.SemaphoreType.DMA((2, 2 * CX))],
        compiler_params=pltpu.CompilerParams(vmem_limit_bytes=32 * 1024 * 1024),
        name="finish",
    )(*state))


def solution(mesh):
    cells = P("sub", "blk", None)
    return jax.shard_map(
        functools.partial(body, mesh), mesh=mesh,
        in_specs=(cells,) * 7 + (P("sub", "blk"), P()), out_specs=(cells, cells), check_vma=False,
    )
```

time: 65.8 us -> 42.7 us (0.65)
  Pallas kernels: 56.1 us -> 41.1 us
  local copies, waits for them, and re-layouts: 8.14 us -> 0 us
    pallas_call x1 -> x2, Pallas kernels: 56.1 us -> 41.1 us  [the longest x1 38.9 us: body(): pl.pallas_call(functools.partial(kernel, n_sub, n_blk), out_shape=(vm(*pa...]
    unnamed x12 -> x0, local copies, waits for them, and re-layouts: 8.14 us -> none
where the time goes in v2:
time: 42.7 us; the launch traced here: 42.6 us
  Pallas kernels  41.1 us (96%)
  between operations  1.45 us (3%)
    pallas_call x1, Pallas kernels, body(): pl.pallas_call(functools.partial(kernel, n_sub, n_blk), out_shape=(vm(*pa...  38.9 us
    pallas_call x1, Pallas kernels, body(): pl.pallas_call(finish_kernel, out_shape=(like(*block), like(*block)), in_...  2.23 us

profile of v2, /device:TPU:1, one launch (start us, length us, event | category | flops | bytes accessed | tf_op | source)
XLA Modules:
  0.0 42.6 jit_solution(6757160296818370519)
XLA Ops:
  1.3 38.9 %darcy_cg.1 = (f32[4,272,512]{2,1,0:T(8,128)S(1)}, f32[4,272,512]{2,1,0:T(8,128)S(1)}, f32[4,256,512]{2,1,0:T(8,128)S(1)}, f32[16,128]{1,0:T(8,128)S(1)}) custom-call(f32[4,256,512]{2,1,0:T(8,128)} %b_hbm.1, f32[4,256,512]{2,1,0:T(8,128)} %tx_hbm.1, f32[4,256,512]{2,1,0:T(8,128)} %ty_hbm.1, f32[4,256,512]{2,1,0:T(8,128)} %tz_hbm.1, f32[4,256,512]{2,1,0:T(8,128)} %st_hbm.1, ...), custom_call_target="tpu_custom_call" | custom-call | tf_op jit(solution)/shard_map/darcy_cg/pallas_call | solution.py:525
  40.2 2.2 %finish.1 = (f32[4,256,512]{2,1,0:T(8,128)}, f32[4,256,512]{2,1,0:T(8,128)}) custom-call(f32[4,272,512]{2,1,0:T(8,128)S(1)} %get-tuple-element.6.B, f32[4,272,512]{2,1,0:T(8,128)S(1)} %get-tuple-element.7.W, f32[4,256,512]{2,1,0:T(8,128)S(1)} %get-tuple-element.8.V, f32[16,128]{1,0:T(8,128)S(1)} %get-tuple-element.9.scalars), custom_call_target="tpu_custom_call" | custom-call | tf_op jit(solution)/shard_map/finish/pallas_call | solution.py:536

commit v3 on v2

--- a/solution.py
+++ b/solution.py
@@ -37,23 +37,37 @@
 def kernel(n_sub, n_blk, b_hbm, tx_hbm, ty_hbm, tz_hbm, st_hbm, perm_hbm, type_hbm, proj_hbm, count_s,
            B, W, V, scalars,
            TX, TY, TZ, ST,
-           perm_v, type_v, meta, meta_in, PROJ,
+           perm_v, type_v, count_v, perm_in, type_in, count_in, PROJ,
            wpt, wpp, wm, CB, LOW, NAT, GL, GR, GT,
            face_in, last_in, sl, sl_in, psf, psf_in,
            HL, HL2, HJ, ACC, C2L, J1R, C2R,
-           edges, cur, slots,
+           edges, cur, slots, known,
            load_sem, small_sem, ss, rs, ar_ss, ar_rs):
     s, k = lax.axis_index("sub"), lax.axis_index("blk")
     right, left = (lax.rem(s + 1, n_sub), k), (lax.rem(s + n_sub - 1, n_sub), k)
     up, down = (s, lax.rem(k + 1, n_blk)), (s, lax.rem(k + n_blk - 1, n_blk))
     column = [(lax.rem(s + i, n_sub), k) for i in (10, 6, 14, 9, 11, 2, 5, 7, 13, 8, 3, 4, 12, 1, 15)]
     row = [(s, lax.rem(k + i, n_blk)) for i in (4, 3, 5, 2, 6, 1, 7)]
-    near = [column[-2], column[-1], row[-2], row[-1]]
     has_left, has_right, has_down, has_up = s > 0, s < n_sub - 1, k > 0, k < n_blk - 1
 
+    def along(axis, distance):
+        for step in (distance, -distance):
+            here, size = (s, n_sub) if axis == "sub" else (k, n_blk)
+            exists = here + step < size if step > 0 else here + step >= 0
+            yield exists, ((s + step, k) if axis == "sub" else (s, k + step))
+
+    def tell(axis, distance, semaphore):
+        for exists, peer in along(axis, distance):
+            @pl.when(exists)
+            def _():
+                pl.semaphore_signal(semaphore, inc=1, device_id=peer, device_id_type=MESH)
+
+    def hear(axis, distance, semaphore):
+        pl.semaphore_wait(semaphore, sum(exists.astype(I32) for exists, _ in along(axis, distance)))
+
     barrier = pltpu.get_barrier_semaphore()
-    for peer in near + column[:-2] + row[:-2]:
-        pl.semaphore_signal(barrier, inc=1, device_id=peer, device_id_type=MESH)
+    tell("sub", 1, barrier)
+    tell("blk", 1, barrier)
 
     small = [
         pltpu.make_async_copy(perm_hbm, perm_v, small_sem.at[0]),
@@ -76,7 +90,8 @@
 
     @pl.when(s == 0)
     def _():
-        meta_in[...] = jnp.zeros_like(meta_in)
+        for ref in (perm_in, type_in, count_in):
+            ref[...] = jnp.zeros_like(ref)
         last_in[...] = jnp.zeros_like(last_in)
         sl_in[...] = jnp.zeros_like(sl_in)
 
@@ -95,14 +110,9 @@
         for n in (1, 4):
             edges[n] = jnp.zeros((CX, 8, CZ), F32)
 
-    for c in small:
-        c.wait()
-    meta[0:1, :] = perm_v[0]
-    meta[1:2, :] = type_v[0]
-    meta[2:3, :] = jnp.full((1, NFB), count_s[0, 0], I32)
-    meta[3:8, :] = jnp.zeros((5, NFB), I32)
-
-    pl.semaphore_wait(barrier, n_sub + n_blk - 2)
+    count_v[...] = jnp.full((8, FB), count_s[0, 0], I32)
+
+    pl.semaphore_wait(barrier, sum(e.astype(I32) for e in (has_left, has_right, has_down, has_up)))
 
     class Send:
         def __init__(self, src, dst, n, to, sends, receives):
@@ -122,28 +132,38 @@
 
     to_up, to_down = (up, has_up, has_down), (down, has_down, has_up)
     to_right, to_left = (right, has_right, has_left), (left, has_left, has_right)
-    b_up = Send(b_hbm.at[:, CY - 1 : CY, :], edges.at[0, :, 0:1, :], 0, *to_up)
-    b_down = Send(b_hbm.at[:, 0:1, :], edges.at[1, :, 0:1, :], 1, *to_down)
-    ty_up = Send(ty_hbm.at[:, CY - 1 : CY, :], edges.at[2, :, 0:1, :], 2, *to_up)
-    meta_right = Send(meta, meta_in, 3, *to_right)
-    w_up = Send(W.at[:, PAD + CY - 1 : PAD + CY, :], edges.at[3, :, 0:1, :], 4, *to_up)
-    w_down = Send(W.at[:, PAD : PAD + 1, :], edges.at[4, :, 0:1, :], 5, *to_down)
+    pairs_right = [Send(perm_hbm, perm_in, 0, *to_right), Send(type_hbm, type_in, 1, *to_right),
+                   Send(count_v, count_in, 2, *to_right)]
+    b_up = Send(b_hbm.at[:, CY - 1 : CY, :], edges.at[0, :, 0:1, :], 3, *to_up)
+    b_down = Send(b_hbm.at[:, 0:1, :], edges.at[1, :, 0:1, :], 4, *to_down)
+    ty_up = Send(ty_hbm.at[:, CY - 1 : CY, :], edges.at[2, :, 0:1, :], 5, *to_up)
+
+    def w_edges(at, n):
+        return [Send(W.at[at, PAD + CY - 1 : PAD + CY, :], edges.at[3, at, 0:1, :], n, *to_up),
+                Send(W.at[at, PAD : PAD + 1, :], edges.at[4, at, 0:1, :], n + 1, *to_down)]
+
+    w_inner, w_first, w_last = w_edges(pl.ds(1, 2), 6), w_edges(pl.ds(0, 1), 8), w_edges(pl.ds(3, 1), 10)
     quarter = [pl.ds(q * CY, CY) for q in range(GROUPS)]
-    sl_right = [Send(sl.at[quarter[q]], sl_in.at[quarter[q]], 6 + q, *to_right) for q in range(GROUPS)]
-    psf_left = [Send(psf.at[quarter[q]], psf_in.at[quarter[q]], 10 + q, *to_left) for q in range(GROUPS)]
+    sl_right = [Send(sl.at[quarter[q]], sl_in.at[quarter[q]], 12 + q, *to_right) for q in range(GROUPS)]
+    psf_left = [Send(psf.at[quarter[q]], psf_in.at[quarter[q]], 16 + q, *to_left) for q in range(GROUPS)]
     parts = [pl.ds(0, CY - BAND), pl.ds(CY - BAND, BAND)]
-    first_left = [Send(b_hbm.at[0, p], face_in.at[p], 14 + n, *to_left) for n, p in enumerate(parts)]
-    last_right = [Send(b_hbm.at[CX - 1, p], last_in.at[p], 16 + n, *to_right) for n, p in enumerate(parts)]
-
+    first_left = [Send(b_hbm.at[0, p], face_in.at[p], 20 + n, *to_left) for n, p in enumerate(parts)]
+    last_right = [Send(b_hbm.at[CX - 1, p], last_in.at[p], 22 + n, *to_right) for n, p in enumerate(parts)]
+
+    for c in pairs_right:
+        c.start()
+    for n in range(2):
+        first_left[n].start()
+        last_right[n].start()
     b_up.start()
     b_down.start()
     ty_up.start()
-    meta_right.start()
-    for n in range(2):
-        first_left[n].start()
-        last_right[n].start()
+    tell("sub", 1, known.at[0])
+    tell("blk", 1, known.at[4])
     for key in order[6:]:
         loads[key].start()
+    for c in small:
+        c.wait()
 
     def place_matrix(target, t, matrix):
         high = matrix.astype(BF16)
@@ -163,16 +183,16 @@
     lane = lax.broadcasted_iota(I32, (FB, FB), 1)
     sub_row = lax.broadcasted_iota(I32, (FB, FB), 0)
 
-    def columns_of(m, side):
-        perm = m[0:1, :]
-        y = lax.shift_right_logical(perm, 2)
-        place = (lax.shift_right_logical(y, 6) * CY + jnp.bitwise_and(perm, GROUPS - 1) * BAND
-                 + jnp.bitwise_and(y, BAND - 1))
-        live = (lax.broadcasted_iota(I32, (1, NFB), 1) < m[2:3, :]).astype(I32)
-        code = (place + m[1:2, :] * NFB + live * (NFB * KINDS)).astype(F32)
+    def columns_of(perm_ref, type_ref, count_ref, side):
         for i in range(NFB // FB):
-            part = jnp.broadcast_to(code[:, i * FB : (i + 1) * FB], (FB, FB))
-            NAT[i * FB : (i + 1) * FB, :] = part.T
+            at = slice(i * FB, (i + 1) * FB)
+            perm = perm_ref[0, :, at]
+            y = lax.shift_right_logical(perm, 2)
+            place = (lax.shift_right_logical(y, 6) * CY + jnp.bitwise_and(perm, GROUPS - 1) * BAND
+                     + jnp.bitwise_and(y, BAND - 1))
+            live = (lax.broadcasted_iota(I32, (1, FB), 1) + i * FB < count_ref[0:1, :]).astype(I32)
+            code = (place + type_ref[0, :, at] * NFB + live * (NFB * KINDS)).astype(F32)
+            NAT[at, :] = jnp.broadcast_to(code, (FB, FB)).T
         for n in range(GROUPS * GROUPS):
             at = slice(n * BAND, (n + 1) * BAND)
             c = NAT[pl.ds((n // GROUPS) * CY + n % GROUPS, BAND, stride=GROUPS), :].astype(I32)
@@ -217,7 +237,7 @@
         odd = jnp.bitwise_and(CB[side, at, :], NFB) != 0
         return jnp.where(odd, y[:, FB:], y[:, :FB])
 
-    columns_of(meta, 0)
+    columns_of(perm_v, type_v, count_v, 0)
     one_hot(0, GL)
 
     def stencil(S, i, c):
@@ -286,6 +306,11 @@
     for q in (2, 3, 0, 1):
         sl_right[q].start()
 
+    hear("sub", 1, known.at[0])
+    tell("sub", 2, known.at[1])
+    hear("blk", 1, known.at[4])
+    tell("blk", 2, known.at[5])
+
     for a, i in order[6:12]:
         loads[a, i].wait()
     prepare(0)
@@ -303,13 +328,18 @@
 
     lax.fori_loop(0, CY // ROWS, first_face, 0)
 
-    meta_right.wait_recv()
-    columns_of(meta_in, 1)
+    for c in pairs_right:
+        c.wait_recv()
+    columns_of(perm_in, type_in, count_in, 1)
     one_hot(1, GR)
     g = jnp.dot(GR[...], HL2[...], preferred_element_type=F32).astype(BF16)
     psf[...] = project(g, wpt, 1)
     for q in range(GROUPS):
         psf_left[q].start()
+    hear("sub", 2, known.at[1])
+    tell("sub", 4, known.at[2])
+    hear("blk", 2, known.at[5])
+    tell("blk", 4, known.at[6])
     g = jnp.dot(GR[...], HL[...], preferred_element_type=F32).astype(BF16)
     J1R[...] = project(g, wpt, 1)
 
@@ -328,6 +358,11 @@
             return acc[0] + fold(mid * mid), acc[1] + fold(mid * out), acc[2] + fold(out * out)
 
         sums = lax.fori_loop(0, CY // ROWS, middle, sums)
+    for c in w_inner:
+        c.start()
+    hear("sub", 4, known.at[2])
+    tell("sub", 8, known.at[3])
+    hear("blk", 4, known.at[6])
     wv = energy(1, True)(zero)
     wv = energy(2, False)(wv)
 
@@ -361,6 +396,8 @@
         W[0, ys, cols] = w
         mid = B[0, ys, cols]
         sums = sums[0] + fold(mid * mid), sums[1] + fold(mid * w), sums[2] + fold(w * w)
+    for c in w_first:
+        c.start()
     g = ACC[...] + gather_right((3,), rest)
     projected = project(g.astype(BF16), wpt, 0)
     for at, _, cols, ys in pieces(range(GROUPS)):
@@ -372,8 +409,8 @@
         C2L[at, :] = w
         sums = sums[0] + fold(mid * mid), sums[1] + fold(mid * w), sums[2] + fold(w * w)
 
-    w_up.start()
-    w_down.start()
+    for c in w_last:
+        c.start()
 
     C2L[...] = C2L[...] + (PENALTY * right_one) * project(HL[...], wm, 0)
     C2R[...] = C2R[...] + PENALTY * project(HJ[...], wm, 1)
@@ -386,9 +423,10 @@
             psf_left[q].wait_recv()
         return live_of(0, at) * (C2L[at, :] - psf_in[at, :])
 
-    def right_jump(q):
+    def right_jump(q, wait=True):
         at = slice(q * CY, (q + 1) * CY)
-        sl_right[q].wait_recv()
+        if wait:
+            sl_right[q].wait_recv()
         return left_one * live_of(1, at) * (sl_in[at, :] + C2R[at, :])
 
     def add_left(q, jump):
@@ -401,71 +439,65 @@
         for rows, ys, cols, _ in pieces(range(GROUPS)):
             V[0, ys, cols] = V[0, ys, cols] - PENALTY * (g[rows, :FB] + g[rows, FB:])
 
-    no_right = 1.0 - right_one
     mortar = zero
     for q in (2, 3):
         at = slice(q * CY, (q + 1) * CY)
         only = live_of(0, at) * C2L[at, :]
-        mortar = mortar + no_right * fold(only * only)
-    for q in (0, 1):
-        jump = left_jump(q)
-        mortar = mortar + fold(jump * jump)
-    for q in (2, 3):
-        jump = right_jump(q)
-        HJ[q * CY : (q + 1) * CY, :] = split(jump)
-        mortar = mortar + fold(jump * jump)
-    wv = wv + PENALTY * mortar
-
-    w_up.wait_recv()
-    w_down.wait_recv()
+        mortar = mortar + (1.0 - right_one) * fold(only * only)
+    hear("sub", 8, known.at[3])
+    for c in w_inner + w_first + w_last:
+        c.wait_recv()
     across = jnp.zeros((1, CZ), F32)
     for i in range(CX):
         d = W[i, PAD + CY - 1 : PAD + CY, :] - edges[4, i, 0:1, :]
         across = across + TY[i, PAD + CY - 1 : PAD + CY, :] * d * d
         W[i, PAD - 1 : PAD, :] = edges[3, i, 0:1, :]
         W[i, PAD + CY : PAD + CY + 1, :] = edges[4, i, 0:1, :]
-
-    lane_row = lax.broadcasted_iota(I32, (1, 128), 1)
-    packed = jnp.zeros((1, 128), F32)
-    for n, part in enumerate((sums[0], sums[1], sums[2])):
+    lane_row = lax.broadcasted_iota(I32, (1, FB), 1)
+    packed = jnp.zeros((1, FB), F32)
+    for n, part in enumerate(sums):
         packed = jnp.where(lane_row == n, jnp.sum(part), packed)
     packed = jnp.where(lane_row == 3, jnp.sum(wv) + jnp.sum(across), packed)
-    cur[0, 0:1, :] = packed
-
-    def spread(stage, peers):
-        for i, peer in enumerate(peers):
+    for n in range(2):
+        jump = left_jump(n)
+        mortar = mortar + fold(jump * jump)
+        jump = right_jump(2 + n)
+        mortar = mortar + fold(jump * jump)
+
+    def spread(stage, part, peers):
+        cur[stage, 0:1, :] = part
+        for n, peer in enumerate(peers):
             pltpu.make_async_remote_copy(
-                src_ref=cur.at[stage, 0:1], dst_ref=slots.at[stage, i : i + 1],
+                src_ref=cur.at[stage, 0:1], dst_ref=slots.at[stage, n : n + 1],
                 send_sem=ar_ss.at[stage], recv_sem=ar_rs.at[stage], device_id=peer, device_id_type=MESH,
             ).start()
-        return len(peers)
-
-    def collect(stage, count):
-        arrived = slots.at[stage, 0:count]
+
+    def collect(stage, peers):
+        arrived = slots.at[stage, 0 : len(peers)]
         pltpu.make_async_copy(arrived, arrived, ar_rs.at[stage]).wait()
-        return cur[stage, 0:1, :] + jnp.sum(slots[stage, 0:count, :], axis=0, keepdims=True)
-
-    n0 = spread(0, column)
-
-    for i in (3, 0, 1, 2):
+        return cur[stage, 0:1, :] + jnp.sum(slots[stage, 0 : len(peers), :], axis=0, keepdims=True)
+
+    spread(0, jnp.where(lane_row == 3, packed + PENALTY * jnp.sum(mortar), packed), row)
+
+    for i in range(CX):
         def second(c, _, i=i):
             mid, out, inner, here = stencil(W, i, c)
             V[i, here, :] = out
             return 0
+
         lax.fori_loop(0, CY // ROWS, second, 0)
+
     for q in (0, 1):
         add_left(q, left_jump(q, wait=False))
-    add_right(HJ[2 * CY :, :], slice(2 * CY, 4 * CY))
-
-    cur[1, 0:1, :] = collect(0, n0)
-    n1 = spread(1, row)
+    add_right(jnp.concatenate([split(right_jump(q, wait=False)) for q in (2, 3)], axis=0), slice(2 * CY, 4 * CY))
+
+    spread(1, collect(0, row), column)
 
     for q in (2, 3):
         add_left(q, left_jump(q))
-    for q in (0, 1):
-        add_right(split(right_jump(q)), slice(q * CY, (q + 1) * CY))
-
-    total = collect(1, n1)
+        add_right(split(right_jump(q - 2)), slice((q - 2) * CY, (q - 1) * CY))
+
+    total = collect(1, column)
     bb, bw, ww, wv = (total[0:1, n : n + 1] for n in range(4))
     alpha = bb / bw
     rr = alpha * alpha * ww - bb
@@ -475,10 +507,10 @@
     scalars[0:8, :] = jnp.broadcast_to(alpha + alpha2 * (1.0 + beta), (8, 128))
     scalars[8:16, :] = jnp.broadcast_to(alpha * alpha2, (8, 128))
 
-    for c in [b_up, b_down, ty_up, meta_right, w_up, w_down] + first_left + last_right + sl_right + psf_left:
+    for c in pairs_right + [b_up, b_down, ty_up] + w_inner + w_first + w_last + first_left + last_right + sl_right + psf_left:
         c.wait_send()
-    for stage, count in ((0, n0), (1, n1)):
-        sent = slots.at[stage, 0:count]
+    for stage, peers in enumerate((row, column)):
+        sent = slots.at[stage, 0 : len(peers)]
         pltpu.make_async_copy(sent, sent, ar_ss.at[stage]).wait()
 
 
@@ -507,16 +539,17 @@
     scratch = [
         vm(*block), vm(CX, CY + PAD, CZ), vm(*block), vm(*block),
         vm(1, 1, NFB, dtype=I32), vm(1, 1, NFB, dtype=I32),
-        vm(8, NFB, dtype=I32), vm(8, NFB, dtype=I32), vm(KINDS, FB, FB),
+        vm(8, FB, dtype=I32),
+        vm(1, 1, NFB, dtype=I32), vm(1, 1, NFB, dtype=I32), vm(8, FB, dtype=I32), vm(KINDS, FB, FB),
         vm(6 * FB, 2 * FB, dtype=BF16), vm(6 * FB, 2 * FB, dtype=BF16), vm(6 * FB, 2 * FB, dtype=BF16),
         vm(2, NFB, FB, dtype=I32), vm(2, NFB, FB, dtype=BF16), vm(*face),
         vm(NFB, NFB, dtype=BF16), vm(NFB, NFB, dtype=BF16), vm(NFB, NFB, dtype=BF16),
         vm(CY, CZ), vm(CY, CZ), vm(*face), vm(*face), vm(*face), vm(*face),
         vm(NFB, 2 * FB, dtype=BF16), vm(NFB, 2 * FB, dtype=BF16), vm(NFB, 2 * FB, dtype=BF16), vm(NFB, 2 * FB),
         vm(*face), vm(*face), vm(*face),
-        vm(5, CX, 8, CZ), vm(2, 8, 128), vm(2, 16, 128),
+        vm(5, CX, 8, CZ), vm(2, 8, FB), vm(2, n_sub, FB), pltpu.SemaphoreType.REGULAR((7,)),
         pltpu.SemaphoreType.DMA((5, CX)), pltpu.SemaphoreType.DMA((3,)),
-        pltpu.SemaphoreType.DMA((18,)), pltpu.SemaphoreType.DMA((18,)),
+        pltpu.SemaphoreType.DMA((24,)), pltpu.SemaphoreType.DMA((24,)),
         pltpu.SemaphoreType.DMA((2,)), pltpu.SemaphoreType.DMA((2,)),
     ]
     like = lambda *shape: jax.ShapeDtypeStruct(shape, F32)

time: 42.7 us -> 40.3 us (0.944)
  Pallas kernels: 41.1 us -> 38.6 us
    pallas_call x1, Pallas kernels: 38.9 us -> 36.4 us  [body(): pl.pallas_call(functools.partial(kernel, n_sub, n_blk), out_shape=(vm(*pa...]
where the time goes in v3:
time: 40.3 us; the launch traced here: 40.1 us
  Pallas kernels  38.6 us (96%)
  between operations  1.45 us (4%)
    pallas_call x1, Pallas kernels, body(): pl.pallas_call(functools.partial(kernel, n_sub, n_blk), out_shape=(vm(*pa...  36.4 us
    pallas_call x1, Pallas kernels, body(): pl.pallas_call(finish_kernel, out_shape=(like(*block), like(*block)), in_...  2.23 us

profile of v3, /device:TPU:1, one launch (start us, length us, event | category | flops | bytes accessed | tf_op | source)
XLA Modules:
  0.0 40.1 jit_solution(3712171537419994630)
XLA Ops:
  1.3 36.4 %darcy_cg.1 = (f32[4,272,512]{2,1,0:T(8,128)S(1)}, f32[4,272,512]{2,1,0:T(8,128)S(1)}, f32[4,256,512]{2,1,0:T(8,128)S(1)}, f32[16,128]{1,0:T(8,128)S(1)}) custom-call(f32[4,256,512]{2,1,0:T(8,128)} %b_hbm.1, f32[4,256,512]{2,1,0:T(8,128)} %tx_hbm.1, f32[4,256,512]{2,1,0:T(8,128)} %ty_hbm.1, f32[4,256,512]{2,1,0:T(8,128)} %tz_hbm.1, f32[4,256,512]{2,1,0:T(8,128)} %st_hbm.1, ...), custom_call_target="tpu_custom_call" | custom-call | tf_op jit(solution)/shard_map/darcy_cg/pallas_call | solution.py:558
  37.7 2.2 %finish.1 = (f32[4,256,512]{2,1,0:T(8,128)}, f32[4,256,512]{2,1,0:T(8,128)}) custom-call(f32[4,272,512]{2,1,0:T(8,128)S(1)} %get-tuple-element.6.B, f32[4,272,512]{2,1,0:T(8,128)S(1)} %get-tuple-element.7.W, f32[4,256,512]{2,1,0:T(8,128)S(1)} %get-tuple-element.8.V, f32[16,128]{1,0:T(8,128)S(1)} %get-tuple-element.9.scalars), custom_call_target="tpu_custom_call" | custom-call | tf_op jit(solution)/shard_map/finish/pallas_call | solution.py:569

commit v4 on v3

--- a/solution.py
+++ b/solution.py
@@ -46,8 +46,14 @@
     s, k = lax.axis_index("sub"), lax.axis_index("blk")
     right, left = (lax.rem(s + 1, n_sub), k), (lax.rem(s + n_sub - 1, n_sub), k)
     up, down = (s, lax.rem(k + 1, n_blk)), (s, lax.rem(k + n_blk - 1, n_blk))
-    column = [(lax.rem(s + i, n_sub), k) for i in (10, 6, 14, 9, 11, 2, 5, 7, 13, 8, 3, 4, 12, 1, 15)]
-    row = [(s, lax.rem(k + i, n_blk)) for i in (4, 3, 5, 2, 6, 1, 7)]
+    row = [(s, lax.rem(k + i, n_blk)) for i in range(1, n_blk)]
+    line = 4
+    x, z = lax.rem(s, line), s // line
+    away = lambda d, size: min(d, size - d)
+    plane = [(lax.rem(z + i, n_sub // line) * line + x, lax.rem(k + j, n_blk)) for i, j in sorted(
+        ((i, j) for i in range(n_sub // line) for j in range(n_blk) if i or j),
+        key=lambda o: (-away(o[0], n_sub // line) - away(o[1], n_blk) / 2, o))]
+    in_line = [(z * line + lax.rem(x + i, line), k) for i in (2, 1, 3)]
     has_left, has_right, has_down, has_up = s > 0, s < n_sub - 1, k > 0, k < n_blk - 1
 
     def along(axis, distance):
@@ -303,7 +309,7 @@
         return 0
 
     lax.fori_loop(0, CY // ROWS, last_face, 0)
-    for q in (2, 3, 0, 1):
+    for q in (2, 3):
         sl_right[q].start()
 
     hear("sub", 1, known.at[0])
@@ -334,7 +340,7 @@
     one_hot(1, GR)
     g = jnp.dot(GR[...], HL2[...], preferred_element_type=F32).astype(BF16)
     psf[...] = project(g, wpt, 1)
-    for q in range(GROUPS):
+    for q in (0, 1):
         psf_left[q].start()
     hear("sub", 2, known.at[1])
     tell("sub", 4, known.at[2])
@@ -343,6 +349,8 @@
     g = jnp.dot(GR[...], HL[...], preferred_element_type=F32).astype(BF16)
     J1R[...] = project(g, wpt, 1)
 
+    hear("sub", 4, known.at[2])
+    tell("sub", 8, known.at[3])
     one_hot_back(1, GT)
 
     for a, i in order[12:]:
@@ -360,9 +368,10 @@
         sums = lax.fori_loop(0, CY // ROWS, middle, sums)
     for c in w_inner:
         c.start()
-    hear("sub", 4, known.at[2])
-    tell("sub", 8, known.at[3])
+    hear("sub", 8, known.at[3])
     hear("blk", 4, known.at[6])
+    for peer in row:
+        pl.semaphore_signal(known.at[7], inc=1, device_id=peer, device_id_type=MESH)
     wv = energy(1, True)(zero)
     wv = energy(2, False)(wv)
 
@@ -444,7 +453,7 @@
         at = slice(q * CY, (q + 1) * CY)
         only = live_of(0, at) * C2L[at, :]
         mortar = mortar + (1.0 - right_one) * fold(only * only)
-    hear("sub", 8, known.at[3])
+    pl.semaphore_wait(known.at[7], n_blk - 1)
     for c in w_inner + w_first + w_last:
         c.wait_recv()
     across = jnp.zeros((1, CZ), F32)
@@ -477,7 +486,11 @@
         pltpu.make_async_copy(arrived, arrived, ar_rs.at[stage]).wait()
         return cur[stage, 0:1, :] + jnp.sum(slots[stage, 0 : len(peers), :], axis=0, keepdims=True)
 
-    spread(0, jnp.where(lane_row == 3, packed + PENALTY * jnp.sum(mortar), packed), row)
+    spread(0, jnp.where(lane_row == 3, packed + PENALTY * jnp.sum(mortar), packed), plane)
+
+    for q in (0, 1):
+        sl_right[q].start()
+        psf_left[q + 2].start()
 
     for i in range(CX):
         def second(c, _, i=i):
@@ -491,13 +504,13 @@
         add_left(q, left_jump(q, wait=False))
     add_right(jnp.concatenate([split(right_jump(q, wait=False)) for q in (2, 3)], axis=0), slice(2 * CY, 4 * CY))
 
-    spread(1, collect(0, row), column)
+    spread(1, collect(0, plane), in_line)
 
     for q in (2, 3):
         add_left(q, left_jump(q))
         add_right(split(right_jump(q - 2)), slice((q - 2) * CY, (q - 1) * CY))
 
-    total = collect(1, column)
+    total = collect(1, in_line)
     bb, bw, ww, wv = (total[0:1, n : n + 1] for n in range(4))
     alpha = bb / bw
     rr = alpha * alpha * ww - bb
@@ -509,7 +522,7 @@
 
     for c in pairs_right + [b_up, b_down, ty_up] + w_inner + w_first + w_last + first_left + last_right + sl_right + psf_left:
         c.wait_send()
-    for stage, peers in enumerate((row, column)):
+    for stage, peers in enumerate((plane, in_line)):
         sent = slots.at[stage, 0 : len(peers)]
         pltpu.make_async_copy(sent, sent, ar_ss.at[stage]).wait()
 
@@ -547,7 +560,7 @@
         vm(CY, CZ), vm(CY, CZ), vm(*face), vm(*face), vm(*face), vm(*face),
         vm(NFB, 2 * FB, dtype=BF16), vm(NFB, 2 * FB, dtype=BF16), vm(NFB, 2 * FB, dtype=BF16), vm(NFB, 2 * FB),
         vm(*face), vm(*face), vm(*face),
-        vm(5, CX, 8, CZ), vm(2, 8, FB), vm(2, n_sub, FB), pltpu.SemaphoreType.REGULAR((7,)),
+        vm(5, CX, 8, CZ), vm(2, 8, FB), vm(2, 32, FB), pltpu.SemaphoreType.REGULAR((8,)),
         pltpu.SemaphoreType.DMA((5, CX)), pltpu.SemaphoreType.DMA((3,)),
         pltpu.SemaphoreType.DMA((24,)), pltpu.SemaphoreType.DMA((24,)),
         pltpu.SemaphoreType.DMA((2,)), pltpu.SemaphoreType.DMA((2,)),

time: 40.3 us -> 39.2 us (0.973)
  Pallas kernels: 38.6 us -> 37.5 us
    pallas_call x1, Pallas kernels: 36.4 us -> 35.2 us  [body(): pl.pallas_call(functools.partial(kernel, n_sub, n_blk), out_shape=(vm(*pa...]
where the time goes in v4:
time: 39.2 us; the launch traced here: 38.9 us
  Pallas kernels  37.5 us (96%)
  between operations  1.45 us (4%)
    pallas_call x1, Pallas kernels, body(): pl.pallas_call(functools.partial(kernel, n_sub, n_blk), out_shape=(vm(*pa...  35.2 us
    pallas_call x1, Pallas kernels, body(): pl.pallas_call(finish_kernel, out_shape=(like(*block), like(*block)), in_...  2.23 us

profile of v4, /device:TPU:1, one launch (start us, length us, event | category | flops | bytes accessed | tf_op | source)
XLA Modules:
  0.0 38.9 jit_solution(8629337731614269083)
XLA Ops:
  1.3 35.2 %darcy_cg.1 = (f32[4,272,512]{2,1,0:T(8,128)S(1)}, f32[4,272,512]{2,1,0:T(8,128)S(1)}, f32[4,256,512]{2,1,0:T(8,128)S(1)}, f32[16,128]{1,0:T(8,128)S(1)}) custom-call(f32[4,256,512]{2,1,0:T(8,128)} %b_hbm.1, f32[4,256,512]{2,1,0:T(8,128)} %tx_hbm.1, f32[4,256,512]{2,1,0:T(8,128)} %ty_hbm.1, f32[4,256,512]{2,1,0:T(8,128)} %tz_hbm.1, f32[4,256,512]{2,1,0:T(8,128)} %st_hbm.1, ...), custom_call_target="tpu_custom_call" | custom-call | tf_op jit(solution)/shard_map/darcy_cg/pallas_call | solution.py:571
  36.5 2.2 %finish.1 = (f32[4,256,512]{2,1,0:T(8,128)}, f32[4,256,512]{2,1,0:T(8,128)}) custom-call(f32[4,272,512]{2,1,0:T(8,128)S(1)} %get-tuple-element.6.B, f32[4,272,512]{2,1,0:T(8,128)S(1)} %get-tuple-element.7.W, f32[4,256,512]{2,1,0:T(8,128)S(1)} %get-tuple-element.8.V, f32[16,128]{1,0:T(8,128)S(1)} %get-tuple-element.9.scalars), custom_call_target="tpu_custom_call" | custom-call | tf_op jit(solution)/shard_map/finish/pallas_call | solution.py:582

commit v5 on v4

--- a/solution.py
+++ b/solution.py
@@ -94,28 +94,6 @@
     for key in order[:6]:
         loads[key].start()
 
-    @pl.when(s == 0)
-    def _():
-        for ref in (perm_in, type_in, count_in):
-            ref[...] = jnp.zeros_like(ref)
-        last_in[...] = jnp.zeros_like(last_in)
-        sl_in[...] = jnp.zeros_like(sl_in)
-
-    @pl.when(s == n_sub - 1)
-    def _():
-        face_in[...] = jnp.zeros_like(face_in)
-        psf_in[...] = jnp.zeros_like(psf_in)
-
-    @pl.when(k == 0)
-    def _():
-        for n in (0, 2, 3):
-            edges[n] = jnp.zeros((CX, 8, CZ), F32)
-
-    @pl.when(k == n_blk - 1)
-    def _():
-        for n in (1, 4):
-            edges[n] = jnp.zeros((CX, 8, CZ), F32)
-
     count_v[...] = jnp.full((8, FB), count_s[0, 0], I32)
 
     pl.semaphore_wait(barrier, sum(e.astype(I32) for e in (has_left, has_right, has_down, has_up)))
@@ -170,6 +148,28 @@
         loads[key].start()
     for c in small:
         c.wait()
+
+    @pl.when(s == 0)
+    def _():
+        for ref in (perm_in, type_in, count_in):
+            ref[...] = jnp.zeros_like(ref)
+        last_in[...] = jnp.zeros_like(last_in)
+        sl_in[...] = jnp.zeros_like(sl_in)
+
+    @pl.when(s == n_sub - 1)
+    def _():
+        face_in[...] = jnp.zeros_like(face_in)
+        psf_in[...] = jnp.zeros_like(psf_in)
+
+    @pl.when(k == 0)
+    def _():
+        for n in (0, 2, 3):
+            edges[n] = jnp.zeros((CX, 8, CZ), F32)
+
+    @pl.when(k == n_blk - 1)
+    def _():
+        for n in (1, 4):
+            edges[n] = jnp.zeros((CX, 8, CZ), F32)
 
     def place_matrix(target, t, matrix):
         high = matrix.astype(BF16)

time: 39.2 us -> 39.2 us (level)
  no operation moved by 1% of the time
where the time goes in v5:
time: 39.2 us; the launch traced here: 38.9 us
  Pallas kernels  37.5 us (96%)
  between operations  1.45 us (4%)
    pallas_call x1, Pallas kernels, body(): pl.pallas_call(functools.partial(kernel, n_sub, n_blk), out_shape=(vm(*pa...  35.2 us
    pallas_call x1, Pallas kernels, body(): pl.pallas_call(finish_kernel, out_shape=(like(*block), like(*block)), in_...  2.23 us

profile of v5, /device:TPU:1, one launch (start us, length us, event | category | flops | bytes accessed | tf_op | source)
XLA Modules:
  0.0 38.9 jit_solution(6577932200644304290)
XLA Ops:
  1.3 35.2 %darcy_cg.1 = (f32[4,272,512]{2,1,0:T(8,128)S(1)}, f32[4,272,512]{2,1,0:T(8,128)S(1)}, f32[4,256,512]{2,1,0:T(8,128)S(1)}, f32[16,128]{1,0:T(8,128)S(1)}) custom-call(f32[4,256,512]{2,1,0:T(8,128)} %b_hbm.1, f32[4,256,512]{2,1,0:T(8,128)} %tx_hbm.1, f32[4,256,512]{2,1,0:T(8,128)} %ty_hbm.1, f32[4,256,512]{2,1,0:T(8,128)} %tz_hbm.1, f32[4,256,512]{2,1,0:T(8,128)} %st_hbm.1, ...), custom_call_target="tpu_custom_call" | custom-call | tf_op jit(solution)/shard_map/darcy_cg/pallas_call | solution.py:571
  36.5 2.2 %finish.1 = (f32[4,256,512]{2,1,0:T(8,128)}, f32[4,256,512]{2,1,0:T(8,128)}) custom-call(f32[4,272,512]{2,1,0:T(8,128)S(1)} %get-tuple-element.6.B, f32[4,272,512]{2,1,0:T(8,128)S(1)} %get-tuple-element.7.W, f32[4,256,512]{2,1,0:T(8,128)S(1)} %get-tuple-element.8.V, f32[16,128]{1,0:T(8,128)S(1)} %get-tuple-element.9.scalars), custom_call_target="tpu_custom_call" | custom-call | tf_op jit(solution)/shard_map/finish/pallas_call | solution.py:582
